TPU v7x, 32 devices: a whole 2x2x4 slice. The times are simulated.
32 devices in a mesh: row: 4 (over y, core), seq: 8 (over z, x).
Axes of the slice: x: 2, y: 2, z: 4, core: 2. Of those that a mesh axis runs over, the one named last changes fastest.
Arguments:
- activations: bfloat16 [3, 4, 1024, 1024], P(None, 'row', 'seq'), may hold values from -6 to 6
- cotangent: bfloat16 [3, 4, 1024, 1024], P(None, 'row', 'seq'), may hold values from -6 to 6
- segment_ids: int32 [3, 4, 1024], P(None, 'row', 'seq'), may hold values from 0 to 3, never falling along the last dimension, each value on 1 to 512 neighbouring positions
- prefix_embed: float32 [10, 1024], replicated, may hold values from -6 to 6
- adapt_in: float32 [1024, 512], replicated, may hold values from -0.1875 to 0.1875
- adapt_in_bias: float32 [512], replicated, may hold values from -1.8 to 1.8
- adapt_out: float32 [512, 2048], replicated, may hold values from -0.375 to 0.375
- adapt_out_bias: float32 [2048], replicated, may hold values from -1.8 to 1.8
- ln1_gain: bfloat16 [1024], replicated, may hold values from 0.5 to 1.5
- ln1_bias: bfloat16 [1024], replicated, may hold values from -1.796875 to 1.796875
- qkv_weight: bfloat16 [1024, 3072], P('row', 'seq'), may hold values from -0.1875 to 0.1875
- qkv_bias: bfloat16 [3072], replicated, may hold values from -1.796875 to 1.796875
- out_weight: bfloat16 [1024, 1024], P('row', 'seq'), may hold values from -0.75 to 0.75
- out_bias: bfloat16 [1024], replicated, may hold values from -1.796875 to 1.796875
- ln2_gain: bfloat16 [1024], replicated, may hold values from 0.5 to 1.5
- ln2_bias: bfloat16 [1024], replicated, may hold values from -1.796875 to 1.796875
- fc_weight: bfloat16 [1024, 4096], P('row', 'seq'), may hold values from -0.1875 to 0.1875
- fc_bias: bfloat16 [4096], replicated, may hold values from -1.796875 to 1.796875
- proj_weight: bfloat16 [4096, 1024], P('row', 'seq'), may hold values from -0.09375 to 0.09375
- proj_bias: bfloat16 [1024], replicated, may hold values from -1.796875 to 1.796875
Outputs:
- output: bfloat16 [3, 4, 1024, 1024], P(None, 'row', 'seq')
- in_grad: bfloat16 [3, 4, 1024, 1024], P(None, 'row', 'seq')
- prefix_grad: float32 [10, 1024], replicated
- adapt_in_grad: float32 [1024, 512], replicated
- adapt_in_bias_grad: float32 [512], replicated
- adapt_out_grad: float32 [512, 2048], replicated
- adapt_out_bias_grad: float32 [2048], replicated
Inputs may be any that keep to these rules, and one draw needn't show every extreme that they name: `segment_ids`: along every packed row the ids never fall; each document has 1 to 512 tokens and some document has exactly 512.
All inputs are finite; a program needn't handle non-finite values.
Results may differ from a plain program's by a relative error of at most 0.014.
Values may be sent and summed in bfloat16 or wider, within the bound.
No kernel may reach another device: no remote copies, remote signals or barrier semaphores. Data moves between devices by JAX's collectives and lax.ppermute only.
A program may use at most 192 MiB of HBM per device.

v0:
```python
from functools import partial
import math

import jax
import jax.numpy as jnp
from jax import lax
from jax.sharding import PartitionSpec as P

HEADS = 16


masked_fill = -1e30


def passed_along(value, axis, steps):
    count = lax.axis_size(axis)
    initial, last = (max(0, -steps), min(count, count - steps))
    return lax.ppermute(value, axis, [(source, source + steps) for source in range(initial, last)])


def as_sent(shard):

    def short(part):
        return part.astype(jnp.bfloat16) if part.dtype == jnp.float32 else part

    return jax.tree.map(short, shard)


def shifted(value, axis, steps):
    count = lax.axis_size(axis)
    pairs = [(source, (source + steps) % count) for source in range(count)]
    return lax.ppermute(value, axis, pairs)


def matmul_high(left_op, right_op):
    return jnp.dot(
        left_op, right_op, precision=lax.Precision.HIGHEST, preferred_element_type=jnp.float32
    )


def prefix_pairs(prefix_embed, adapt_in, adapt_in_bias, adapt_out, adapt_out_bias):
    squashed = jnp.tanh(matmul_high(prefix_embed, adapt_in) + adapt_in_bias)
    return matmul_high(squashed, adapt_out) + adapt_out_bias


def layer_norm(values, norm_gain, norm_shift):
    centre = values - jnp.mean(values, axis=-1, keepdims=True)
    spread = jnp.mean(centre * centre, axis=-1, keepdims=True)
    return centre * lax.rsqrt(spread + 1e-05) * norm_gain + norm_shift


def gelu_tanh(values):
    return (
        0.5
        * values
        * (1.0 + jnp.tanh(0.7978845608028654 * (values + 0.044715 * values * values * values)))
    )


def dot_transposed(left_op, right_op):
    return lax.dot_general(
        left_op, right_op, (((1,), (1,)), ((), ())), preferred_element_type=jnp.float32
    )


def block_scores(queries, keys_blk, query_seg, key_seg, query_pos, key_pos, score_scale):
    scores = (
        jnp.einsum("rqhd,rkhd->rhqk", queries, keys_blk, preferred_element_type=jnp.float32)
        * score_scale
    )
    allowed = (query_seg[:, :, None] == key_seg[:, None, :]) & (
        key_pos[None, None, :] <= query_pos[None, :, None]
    )
    return jnp.where(allowed[:, None, :, :], scores, masked_fill)


def keep_carry(carry_in):
    return carry_in


def run_block(usable, update_fn, skip_fn, carry_in):
    if usable is None:
        return update_fn(carry_in)
    return lax.cond(usable, update_fn, skip_fn, carry_in)


def attend_forward(queries, blocks, query_seg, query_pos, pre_keys, pre_values, score_scale):
    pre_scores = (
        jnp.einsum("rqhd,phd->rhqp", queries, pre_keys, preferred_element_type=jnp.float32)
        * score_scale
    )
    running_max = jnp.max(pre_scores, axis=-1)
    running_sum = jnp.sum(jnp.exp(pre_scores - running_max[..., None]), axis=-1)
    for keys_blk, values_blk, key_seg, key_pos, usable in blocks:

        def widen(carry_in):
            scores = block_scores(
                queries, keys_blk, query_seg, key_seg, query_pos, key_pos, score_scale
            )
            new_max = jnp.maximum(carry_in[0], jnp.max(scores, axis=-1))
            new_sum = carry_in[1] * jnp.exp(carry_in[0] - new_max) + jnp.sum(
                jnp.exp(scores - new_max[..., None]), axis=-1
            )
            return (new_max, new_sum)

        running_max, running_sum = run_block(usable, widen, keep_carry, (running_max, running_sum))
    log_total = running_max + jnp.log(running_sum)
    pre_probs = jnp.exp(pre_scores - log_total[..., None]).astype(jnp.bfloat16)
    attended = jnp.einsum(
        "rhqp,phd->rqhd", pre_probs, pre_values, preferred_element_type=jnp.float32
    )
    for keys_blk, values_blk, key_seg, key_pos, usable in blocks:

        def collect(accum_in):
            scores = block_scores(
                queries, keys_blk, query_seg, key_seg, query_pos, key_pos, score_scale
            )
            attn_probs = jnp.exp(scores - log_total[..., None]).astype(jnp.bfloat16)
            return accum_in + jnp.einsum(
                "rhqk,rkhd->rqhd", attn_probs, values_blk, preferred_element_type=jnp.float32
            )

        attended = run_block(usable, collect, keep_carry, attended)
    return (attended, log_total)


def attend_backward(
    queries,
    blocks,
    query_seg,
    query_pos,
    pre_keys,
    pre_values,
    score_scale,
    log_total,
    attended,
    grad_att,
):
    row_delta = jnp.einsum("rqhd,rqhd->rhq", grad_att.astype(jnp.float32), attended)
    pre_scores = (
        jnp.einsum("rqhd,phd->rhqp", queries, pre_keys, preferred_element_type=jnp.float32)
        * score_scale
    )
    pre_probs = jnp.exp(pre_scores - log_total[..., None])
    pre_grad_probs = jnp.einsum(
        "rqhd,phd->rhqp", grad_att, pre_values, preferred_element_type=jnp.float32
    )
    pre_grad_scores = (pre_probs * (pre_grad_probs - row_delta[..., None])).astype(jnp.bfloat16)
    grad_q = (
        jnp.einsum("rhqp,phd->rqhd", pre_grad_scores, pre_keys, preferred_element_type=jnp.float32)
        * score_scale
    )
    grad_pre_k = (
        jnp.einsum("rhqp,rqhd->phd", pre_grad_scores, queries, preferred_element_type=jnp.float32)
        * score_scale
    )
    grad_pre_v = jnp.einsum(
        "rhqp,rqhd->phd",
        pre_probs.astype(jnp.bfloat16),
        grad_att,
        preferred_element_type=jnp.float32,
    )
    block_grads = []
    for keys_blk, values_blk, key_seg, key_pos, usable in blocks:

        def contribute(grad_q_old):
            scores = block_scores(
                queries, keys_blk, query_seg, key_seg, query_pos, key_pos, score_scale
            )
            attn_probs = jnp.exp(scores - log_total[..., None])
            grad_probs = jnp.einsum(
                "rqhd,rkhd->rhqk", grad_att, values_blk, preferred_element_type=jnp.float32
            )
            grad_scores = (attn_probs * (grad_probs - row_delta[..., None])).astype(jnp.bfloat16)
            grad_q_new = (
                grad_q_old
                + jnp.einsum(
                    "rhqk,rkhd->rqhd", grad_scores, keys_blk, preferred_element_type=jnp.float32
                )
                * score_scale
            )
            grad_k = (
                jnp.einsum(
                    "rhqk,rqhd->rkhd", grad_scores, queries, preferred_element_type=jnp.float32
                )
                * score_scale
            )
            grad_v = jnp.einsum(
                "rhqk,rqhd->rkhd",
                attn_probs.astype(jnp.bfloat16),
                grad_att,
                preferred_element_type=jnp.float32,
            )
            return (grad_q_new, grad_k, grad_v)

        def skip_grads(grad_q_old):
            empty_grad = jnp.zeros(keys_blk.shape, jnp.float32)
            return (grad_q_old, empty_grad, empty_grad)

        grad_q, grad_k, grad_v = run_block(usable, contribute, skip_grads, grad_q)
        block_grads.append((grad_k, grad_v))
    return (grad_q, block_grads, grad_pre_k, grad_pre_v)


def local(
    activations,
    cotangent,
    segment_ids,
    prefix_embed,
    adapt_in,
    adapt_in_bias,
    adapt_out,
    adapt_out_bias,
    ln1_gain,
    ln1_bias,
    qkv_weight,
    qkv_bias,
    out_weight,
    out_bias,
    ln2_gain,
    ln2_bias,
    fc_weight,
    fc_bias,
    proj_weight,
    proj_bias,
):
    batches, rows_dev, tok_dev, model_width = activations.shape
    head_count = HEADS
    head_size = model_width // head_count
    tokens = rows_dev * tok_dev
    cycle_span = min(4, lax.axis_size("seq") // 2)
    cycle_pos = lax.axis_index("seq")
    score_scale = 1.0 / math.sqrt(head_size)
    query_pos = cycle_pos * tok_dev + jnp.arange(tok_dev, dtype=jnp.int32)
    norm1_gain = ln1_gain.astype(jnp.float32)
    norm1_shift = ln1_bias.astype(jnp.float32)
    norm2_gain = ln2_gain.astype(jnp.float32)
    norm2_shift = ln2_bias.astype(jnp.float32)
    qkv_vec = qkv_bias.astype(jnp.float32)
    out_vec = out_bias.astype(jnp.float32)
    fc_vec = fc_bias.astype(jnp.float32)
    proj_vec = proj_bias.astype(jnp.float32)
    prefix_kv, prefix_back = jax.vjp(
        prefix_pairs, prefix_embed, adapt_in, adapt_in_bias, adapt_out, adapt_out_bias
    )
    prefix_low = prefix_kv.astype(jnp.bfloat16)
    prefix_count = prefix_kv.shape[0]
    pre_keys = prefix_low[:, :model_width].reshape(prefix_count, head_count, head_size)
    pre_values = prefix_low[:, model_width:].reshape(prefix_count, head_count, head_size)
    grad_pre_keys = jnp.zeros((prefix_count, head_count, head_size), jnp.float32)
    grad_pre_values = jnp.zeros((prefix_count, head_count, head_size), jnp.float32)
    outputs = []
    in_grads = []
    for batch_idx in range(batches):
        gathered = (
            lax.all_gather(
                lax.all_gather(qkv_weight, "row", axis=0, tiled=True), "seq", axis=1, tiled=True
            ),
            lax.all_gather(
                lax.all_gather(out_weight, "row", axis=0, tiled=True), "seq", axis=1, tiled=True
            ),
            lax.all_gather(
                lax.all_gather(fc_weight, "row", axis=0, tiled=True), "seq", axis=1, tiled=True
            ),
            lax.all_gather(
                lax.all_gather(proj_weight, "row", axis=0, tiled=True), "seq", axis=1, tiled=True
            ),
        )
        qkv_mat, out_mat, fc_mat, proj_mat = gathered
        row_in = activations[batch_idx].astype(jnp.float32).reshape(tokens, model_width)
        normed_first, norm_back_first = jax.vjp(
            partial(layer_norm, norm_gain=norm1_gain, norm_shift=norm1_shift), row_in
        )
        mixed_qkv = (
            jnp.dot(normed_first.astype(jnp.bfloat16), qkv_mat, preferred_element_type=jnp.float32)
            + qkv_vec
        ).astype(jnp.bfloat16)
        queries = mixed_qkv[:, :model_width].reshape(rows_dev, tok_dev, head_count, head_size)
        keys_home = mixed_qkv[:, model_width : 2 * model_width].reshape(
            rows_dev, tok_dev, head_count, head_size
        )
        values_home = mixed_qkv[:, 2 * model_width :].reshape(
            rows_dev, tok_dev, head_count, head_size
        )
        query_seg = segment_ids[batch_idx]
        blocks = [(keys_home, values_home, query_seg, query_pos, None)]
        keys_blk, values_blk, key_seg = (keys_home, values_home, query_seg)
        for cycle_step in range(1, cycle_span + 1):
            keys_blk, values_blk = passed_along((keys_blk, values_blk), "seq", 1)
            key_seg = passed_along(key_seg, "seq", 1)
            source = cycle_pos - cycle_step
            key_pos = source * tok_dev + jnp.arange(tok_dev, dtype=jnp.int32)
            usable = (source >= 0) & jnp.any(key_seg[:, tok_dev - 1] == query_seg[:, 0])
            blocks.append((keys_blk, values_blk, key_seg, key_pos, usable))
        attended, log_total = attend_forward(
            queries, blocks, query_seg, query_pos, pre_keys, pre_values, score_scale
        )
        attended_low = attended.reshape(tokens, model_width).astype(jnp.bfloat16)
        middle = (
            row_in + jnp.dot(attended_low, out_mat, preferred_element_type=jnp.float32) + out_vec
        )
        normed_second, norm_back_second = jax.vjp(
            partial(layer_norm, norm_gain=norm2_gain, norm_shift=norm2_shift), middle
        )
        hidden_pre = (
            jnp.dot(normed_second.astype(jnp.bfloat16), fc_mat, preferred_element_type=jnp.float32)
            + fc_vec
        )
        hidden, gelu_back = jax.vjp(gelu_tanh, hidden_pre)
        result = (
            middle
            + jnp.dot(hidden.astype(jnp.bfloat16), proj_mat, preferred_element_type=jnp.float32)
            + proj_vec
        )
        outputs.append(result.astype(jnp.bfloat16).reshape(rows_dev, tok_dev, model_width))
        grad_out = cotangent[batch_idx].reshape(tokens, model_width)
        grad_hidden = dot_transposed(grad_out, proj_mat)
        grad_pre = gelu_back(grad_hidden)[0].astype(jnp.bfloat16)
        grad_middle = (
            grad_out.astype(jnp.float32) + norm_back_second(dot_transposed(grad_pre, fc_mat))[0]
        )
        grad_att = dot_transposed(grad_middle.astype(jnp.bfloat16), out_mat).astype(jnp.bfloat16)
        grad_att = grad_att.reshape(rows_dev, tok_dev, head_count, head_size)
        grad_q, block_grads, grad_pre_k, grad_pre_v = attend_backward(
            queries,
            blocks,
            query_seg,
            query_pos,
            pre_keys,
            pre_values,
            score_scale,
            log_total,
            attended,
            grad_att,
        )
        grad_pre_keys = grad_pre_keys + grad_pre_k
        grad_pre_values = grad_pre_values + grad_pre_v
        travel = block_grads[0]
        for cycle_step in range(1, cycle_span + 1):
            travel = shifted((as_sent(travel[0]), as_sent(travel[1])), "seq", 1)
            travel = (
                travel[0] + block_grads[cycle_step][0],
                travel[1] + block_grads[cycle_step][1],
            )
        home_grads = shifted((as_sent(travel[0]), as_sent(travel[1])), "seq", -cycle_span)
        grad_mixed = jnp.concatenate(
            [
                grad_q.reshape(tokens, model_width),
                home_grads[0].reshape(tokens, model_width),
                home_grads[1].reshape(tokens, model_width),
            ],
            axis=1,
        ).astype(jnp.bfloat16)
        grad_in = grad_middle + norm_back_first(dot_transposed(grad_mixed, qkv_mat))[0]
        in_grads.append(grad_in.astype(jnp.bfloat16).reshape(rows_dev, tok_dev, model_width))
    grad_prefix_kv = jnp.concatenate(
        [
            grad_pre_keys.reshape(prefix_count, model_width),
            grad_pre_values.reshape(prefix_count, model_width),
        ],
        axis=1,
    )
    local_grads = prefix_back(grad_prefix_kv)
    summed = lax.psum(
        (local_grads[0], local_grads[1], local_grads[2], local_grads[3], local_grads[4]),
        ("row", "seq"),
    )
    return (
        jnp.stack(outputs),
        jnp.stack(in_grads),
        summed[0],
        summed[1],
        summed[2],
        summed[3],
        summed[4],
    )


def solution(mesh):
    placed = (
        P(None, "row", "seq", None),
        P(None, "row", "seq", None),
        P(None, "row", "seq"),
        P(),
        P(),
        P(),
        P(),
        P(),
        P(),
        P(),
        P("row", "seq"),
        P(),
        P("row", "seq"),
        P(),
        P(),
        P(),
        P("row", "seq"),
        P(),
        P("row", "seq"),
        P(),
    )
    return jax.shard_map(
        local,
        mesh=mesh,
        in_specs=placed,
        out_specs=(
            P(None, "row", "seq", None),
            P(None, "row", "seq", None),
            P(),
            P(),
            P(),
            P(),
            P(),
        ),
        check_vma=False,
    )
```

profile of v0, /device:TPU:0, one launch (start us, length us, event | category | flops | bytes accessed | tf_op | source)
XLA Modules:
  0.0 1071.5 jit_solution(1047832443013359416)
XLA Ops:
  8.8 11.9 %all_gather.16 = bf16[1024,384]{1,0:T(8,128)(2,1)} all-gather(bf16[256,384]{1,0:T(8,128)(2,1)} %param.102), channel_id=1, replica_groups=mesh['row'=4,'seq'=8] {'row'}, dimensions={0}, use_global_device_ids=true | all-gather | bytes 983040 | tf_op jit(solution)/shard_map/all_gather | solution.py:257
  20.8 8.1 all_gather.18
  30.5 18.2 %all-gather.15.cloned.1.call-done = bf16[4096,128]{1,0:T(8,128)(2,1)} async-done(((bf16[1024,128]{1,0:T(8,128)(2,1)}), bf16[4096,128]{1,0:T(8,128)(2,1)}) %all-gather.15.cloned.1.call-update) | async-done | bytes 1048592 | tf_op jit(solution)/shard_map/all_gather | solution.py:266
  112.3 38.6 %all-gather.7.cloned.1.call-done = bf16[1024,3072]{1,0:T(8,128)(2,1)} async-done(((bf16[1024,384]{1,0:T(8,128)(2,1)}), bf16[1024,3072]{1,0:T(8,128)(2,1)}) %all-gather.7.cloned.1.call-update) | async-done | bytes 6291472 | tf_op jit(solution)/shard_map/all_gather | solution.py:256
  198.2 12.6 %collective-permute-start.5 = (bf16[1,128,16,64]{1,3,2,0:T(8,128)(2,1)S(1)}, bf16[1,128,16,64]{1,3,2,0:T(8,128)(2,1)S(1)}, u32[]{:S(2)}, u32[]{:S(2)}) collective-permute-start(bf16[1,128,16,64]{1,3,2,0:T(8,128)(2,1)S(1)} %collective-permute-done.4), channel_id=1, source_target_pairs={{0,1},{1,2},{2,3},{3,4},{4,5},{5,6},{6,7},{8,9},{9,10},{10,11},{11... | collective-permute-start | bytes 786440 | tf_op jit(solution)/shard_map/ppermute | solution.py:18
  210.9 5.9 collective-permute-start.33
  220.8 7.7 collective-permute-start.9
  228.5 5.6 collective-permute-start.18
  234.1 8.0 collective-permute-start.6
  242.3 11.3 %collective-permute-start.30 = (bf16[1,128,16,64]{1,3,2,0:T(8,128)(2,1)}, bf16[1,128,16,64]{1,3,2,0:T(8,128)(2,1)}, u32[]{:S(2)}, u32[]{:S(2)}) collective-permute-start(bf16[1,128,16,64]{1,3,2,0:T(8,128)(2,1)} %collective-permute-done.29), channel_id=1, source_target_pairs={{0,1},{1,2},{2,3},{3,4},{4,5},{5,6},{6,7},{8,9},{9,10},{10,11},{11... | collective-permute-start | bytes 786440 | tf_op jit(solution)/shard_map/ppermute | solution.py:18
  253.5 10.0 collective-permute-start.34
  263.6 11.1 %collective-permute-start.22 = (bf16[1,128,16,64]{1,3,2,0:T(8,128)(2,1)}, bf16[1,128,16,64]{1,3,2,0:T(8,128)(2,1)}, u32[]{:S(2)}, u32[]{:S(2)}) collective-permute-start(bf16[1,128,16,64]{1,3,2,0:T(8,128)(2,1)} %collective-permute-done.21), channel_id=1, source_target_pairs={{0,1},{1,2},{2,3},{3,4},{4,5},{5,6},{6,7},{8,9},{9,10},{10,11},{11... | collective-permute-start | bytes 786440 | tf_op jit(solution)/shard_map/ppermute | solution.py:18
  274.7 11.2 %collective-permute-start.10 = (bf16[1,128,16,64]{1,3,2,0:T(8,128)(2,1)}, bf16[1,128,16,64]{1,3,2,0:T(8,128)(2,1)}, u32[]{:S(2)}, u32[]{:S(2)}) collective-permute-start(bf16[1,128,16,64]{1,3,2,0:T(8,128)(2,1)} %collective-permute-done.9), channel_id=1, source_target_pairs={{0,1},{1,2},{2,3},{3,4},{4,5},{5,6},{6,7},{8,9},{9,10},{10,11},{11... | collective-permute-start | bytes 786440 | tf_op jit(solution)/shard_map/ppermute | solution.py:18
  285.9 11.3 %collective-permute-start.7 = (bf16[1,128,16,64]{1,3,2,0:T(8,128)(2,1)}, bf16[1,128,16,64]{1,3,2,0:T(8,128)(2,1)}, u32[]{:S(2)}, u32[]{:S(2)}) collective-permute-start(bf16[1,128,16,64]{1,3,2,0:T(8,128)(2,1)} %collective-permute-done.6), channel_id=1, source_target_pairs={{0,1},{1,2},{2,3},{3,4},{4,5},{5,6},{6,7},{8,9},{9,10},{10,11},{11... | collective-permute-start | bytes 786440 | tf_op jit(solution)/shard_map/ppermute | solution.py:18
  300.0 8.8 collective-permute-start.31
  308.9 8.6 collective-permute-start.19
  317.5 9.9 collective-permute-start.35
  327.3 8.8 collective-permute-start.23
  336.1 11.2 %collective-permute-start.11 = (bf16[1,128,16,64]{1,3,2,0:T(8,128)(2,1)}, bf16[1,128,16,64]{1,3,2,0:T(8,128)(2,1)}, u32[]{:S(2)}, u32[]{:S(2)}) collective-permute-start(bf16[1,128,16,64]{1,3,2,0:T(8,128)(2,1)} %collective-permute-done.10), channel_id=1, source_target_pairs={{0,1},{1,2},{2,3},{3,4},{4,5},{5,6},{6,7},{8,9},{9,10},{10,11},{11... | collective-permute-start | bytes 786440 | tf_op jit(solution)/shard_map/ppermute | solution.py:18
  350.2 14.1 %collective-permute-done.11 = bf16[1,128,16,64]{1,3,2,0:T(8,128)(2,1)} collective-permute-done((bf16[1,128,16,64]{1,3,2,0:T(8,128)(2,1)}, bf16[1,128,16,64]{1,3,2,0:T(8,128)(2,1)}, u32[]{:S(2)}, u32[]{:S(2)}) %collective-permute-start.11) | collective-permute-done | bytes 262176 | tf_op jit(solution)/shard_map/ppermute | solution.py:18
  381.7 43.3 %all-gather.13.cloned.1.call-done = bf16[1024,4096]{1,0:T(8,128)(2,1)} async-done(((bf16[1024,512]{1,0:T(8,128)(2,1)}), bf16[1024,4096]{1,0:T(8,128)(2,1)}) %all-gather.13.cloned.1.call-update) | async-done | bytes 8388624 | tf_op jit(solution)/shard_map/all_gather | solution.py:262
  425.0 6.1 convolution_add_fusion
  431.1 119.0 %all-gather.17.cloned.1.call-done = bf16[4096,1024]{1,0:T(8,128)(2,1)} async-done(((bf16[4096,128]{1,0:T(8,128)(2,1)}), bf16[4096,1024]{1,0:T(8,128)(2,1)}) %all-gather.17.cloned.1.call-update) | async-done | bytes 8388624 | tf_op jit(solution)/shard_map/all_gather | solution.py:265
  550.1 13.8 %multiply_reduce_fusion = (f32[128]{0:T(128)S(1)}, f32[128,1024]{1,0:T(8,128)}) fusion(f32[128,1024]{1,0:T(8,128)S(1)} %copy-done.23, f32[128]{0:T(128)S(1)} %broadcast_multiply_fusion, f32[1024]{0:T(1024)S(1)} %convert_element_type.659, bf16[1024,4096]{1,0:T(8,128)(2,1)} %all-gather.13.cloned.1.call-done, f32[128,4096]{1,0:T(8,128)} %convolution_add_fusion, ...), kind=kOutput, calls=%fused_computation.841 | convolution fusion | flops 2160590848 | bytes 20190208 | tf_op jit(solution)/shard_map/dot_general | solution.py:61
  576.0 6.0 convolution_add_fusion.1
  582.0 14.0 %multiply_reduce_fusion.1 = (f32[128]{0:T(128)S(1)}, f32[128,1024]{1,0:T(8,128)}) fusion(f32[128,1024]{1,0:T(8,128)S(1)} %copy-done.20, f32[128]{0:T(128)S(1)} %broadcast_multiply_fusion.2, f32[1024]{0:T(1024)S(1)} %convert_element_type.659, bf16[1024,4096]{1,0:T(8,128)(2,1)} %all-gather.13.cloned.1.call-done, f32[128,4096]{1,0:T(8,128)} %convolution_add_fusion.1, ...), kind=kOutput, calls=%fused_computation.852 | convolution fusion | flops 2160590848 | bytes 20190208 | tf_op jit(solution)/shard_map/dot_general | solution.py:61
  608.3 6.1 convolution_add_fusion.2
  614.4 14.0 %multiply_reduce_fusion.2 = (f32[128]{0:T(128)S(1)}, f32[128,1024]{1,0:T(8,128)}) fusion(f32[128,1024]{1,0:T(8,128)} %copy-done.16, f32[128]{0:T(128)S(1)} %broadcast_multiply_fusion.4, f32[1024]{0:T(1024)S(1)} %convert_element_type.659, bf16[1024,4096]{1,0:T(8,128)(2,1)} %all-gather.13.cloned.1.call-done, f32[128,4096]{1,0:T(8,128)} %convolution_add_fusion.2, ...), kind=kOutput, calls=%fused_computation.863 | convolution fusion | flops 2160590848 | bytes 20190208 | tf_op jit(solution)/shard_map/dot_general | solution.py:61
  653.8 6.9 fusion.782
  681.5 9.2 collective-permute-start.51
  700.6 11.2 %collective-permute-start.36 = (bf16[1,128,16,64]{1,3,2,0:T(8,128)(2,1)}, bf16[1,128,16,64]{1,3,2,0:T(8,128)(2,1)}, u32[]{:S(2)}, u32[]{:S(2)}) collective-permute-start(bf16[1,128,16,64]{1,3,2,0:T(8,128)(2,1)} %fusion.501), channel_id=1, source_target_pairs={{0,1},{1,2},{2,3},{3,4},{4,5},{5,6},{6,7},{7,0},{8,9},{9,10},{10,1... | collective-permute-start | bytes 786440 | tf_op jit(solution)/shard_map/ppermute | solution.py:32
  727.2 5.7 fusion.502
  742.8 67.4 %all-reduce = (f32[10,1024]{1,0:T(8,128)}, f32[512]{0:T(512)}, f32[2048]{0:T(1024)}) all-reduce(f32[10,1024]{1,0:T(8,128)S(1)} %fusion.784, f32[512]{0:T(512)S(1)} %copy-done.161, f32[2048]{0:T(1024)S(1)} %copy-done.159), channel_id=1, replica_groups=mesh['row'=4,'seq'=8] {'row','seq'}, use_global_device_ids=true, to_apply=%region_132.133 | all-reduce | flops 12800 | bytes 102400 | tf_op jit(solution)/shard_map/psum | solution.py:364
  830.7 6.2 collective-permute-done.57
  836.9 5.5 collective-permute-done.52
  842.6 5.5 collective-permute-done.47
  848.2 5.5 collective-permute-done.42
  853.8 5.5 collective-permute-done.37
  859.4 5.5 collective-permute-done.63
  870.6 5.5 collective-permute-done.53
  876.3 5.5 collective-permute-done.48
  881.9 5.5 collective-permute-done.43
  887.5 5.5 collective-permute-done.38
  893.1 11.2 %collective-permute-done.59 = bf16[1,128,16,64]{1,3,2,0:T(8,128)(2,1)S(1)} collective-permute-done((bf16[1,128,16,64]{1,3,2,0:T(8,128)(2,1)S(1)}, bf16[1,128,16,64]{1,3,2,0:T(8,128)(2,1)S(1)}, u32[]{:S(2)}, u32[]{:S(2)}) %collective-permute-start.59) | collective-permute-done | bytes 262176 | tf_op jit(solution)/shard_map/ppermute | solution.py:32
  905.8 9.7 collective-permute-done.49
  926.7 29.2 %collective-permute-start.45 = (bf16[1,128,16,64]{1,3,2,0:T(8,128)(2,1)S(1)}, bf16[1,128,16,64]{1,3,2,0:T(8,128)(2,1)S(1)}, u32[]{:S(2)}, u32[]{:S(2)}) collective-permute-start(bf16[1,128,16,64]{1,3,2,0:T(8,128)(2,1)S(1)} %add_convert_fusion.19), channel_id=1, source_target_pairs={{0,4},{1,5},{2,6},{3,7},{4,0},{5,1},{6,2},{7,3},{8,12},{9,13},{10,... | collective-permute-start | bytes 786440 | tf_op jit(solution)/shard_map/ppermute | solution.py:32
  970.0 6.3 collective-permute-done.40
  981.9 74.8 %all-reduce.4.cloned.1.call-done = (f32[1024,512]{0,1:T(8,128)}, f32[512,2048]{1,0:T(8,128)}) async-done(((f32[1024,512]{0,1:T(8,128)}, f32[512,2048]{1,0:T(8,128)}), (f32[1024,512]{0,1:T(8,128)}, f32[512,2048]{1,0:T(8,128)})) %all-reduce.4.cloned.1.call-update) | async-done | bytes 6291472 | tf_op jit(solution)/shard_map/psum | solution.py:364
  (858 shorter events, 305.3 us)
Async XLA Ops:
  7.9 40.8 %all-gather.15.cloned.1.call-start = ((), (), s32[]{:S(2)}) async-start(), calls=%async_computation.4 | async-start | bytes 1310720 | tf_op jit(solution)/shard_map/all_gather | solution.py:266
  8.8 142.1 %all-gather.7.cloned.1.call-start = ((), (), s32[]{:S(2)}) async-start(), calls=%async_computation | async-start | bytes 7077888 | tf_op jit(solution)/shard_map/all_gather | solution.py:256
  20.7 355.6 %all-gather.9.cloned.1.call-start = ((), (), s32[]{:S(2)}) async-start(), calls=%async_computation.1 | async-start | bytes 2359296 | tf_op jit(solution)/shard_map/all_gather | solution.py:259
  28.9 396.1 %all-gather.13.cloned.1.call-start = ((), (), s32[]{:S(2)}) async-start(), calls=%async_computation.3 | async-start | bytes 9437184 | tf_op jit(solution)/shard_map/all_gather | solution.py:262
  30.5 519.6 %all-gather.17.cloned.1.call-start = ((), (), s32[]{:S(2)}) async-start(), calls=%async_computation.5 | async-start | bytes 9437184 | tf_op jit(solution)/shard_map/all_gather | solution.py:265
  48.8 1007.8 %all-reduce.4.cloned.1.call-start = ((), (), s32[]{:S(2)}) async-start(), calls=%async_computation.6 | async-start | bytes 12582912 | tf_op jit(solution)/shard_map/psum | solution.py:364
  156.8 33.5 %collective-permute-start.28 = (bf16[1,128,16,64]{1,3,2,0:T(8,128)(2,1)}, bf16[1,128,16,64]{1,3,2,0:T(8,128)(2,1)}, u32[]{:S(2)}, u32[]{:S(2)}) collective-permute-start(bf16[1,128,16,64]{1,3,2,0:T(8,128)(2,1)} %bitcast.475), channel_id=1, source_target_pairs={{0,1},{1,2},{2,3},{3,4},{4,5},{5,6},{6,7},{8,9},{9,10},{10,11},{11... | collective-permute-start | bytes 786440 | tf_op jit(solution)/shard_map/ppermute | solution.py:18
  160.9 32.8 %collective-permute-start.32 = (bf16[1,128,16,64]{1,3,2,0:T(8,128)(2,1)}, bf16[1,128,16,64]{1,3,2,0:T(8,128)(2,1)}, u32[]{:S(2)}, u32[]{:S(2)}) collective-permute-start(bf16[1,128,16,64]{1,3,2,0:T(8,128)(2,1)} %bitcast.483), channel_id=1, source_target_pairs={{0,1},{1,2},{2,3},{3,4},{4,5},{5,6},{6,7},{8,9},{9,10},{10,11},{11... | collective-permute-start | bytes 786440 | tf_op jit(solution)/shard_map/ppermute | solution.py:18
  170.8 40.1 %collective-permute-start.20 = (bf16[1,128,16,64]{1,3,2,0:T(8,128)(2,1)}, bf16[1,128,16,64]{1,3,2,0:T(8,128)(2,1)}, u32[]{:S(2)}, u32[]{:S(2)}) collective-permute-start(bf16[1,128,16,64]{1,3,2,0:T(8,128)(2,1)} %bitcast.455), channel_id=1, source_target_pairs={{0,1},{1,2},{2,3},{3,4},{4,5},{5,6},{6,7},{8,9},{9,10},{10,11},{11... | collective-permute-start | bytes 786440 | tf_op jit(solution)/shard_map/ppermute | solution.py:18
  196.8 31.7 %collective-permute-start.17 = (bf16[1,128,16,64]{1,3,2,0:T(8,128)(2,1)}, bf16[1,128,16,64]{1,3,2,0:T(8,128)(2,1)S(1)}, u32[]{:S(2)}, u32[]{:S(2)}) collective-permute-start(bf16[1,128,16,64]{1,3,2,0:T(8,128)(2,1)} %collective-permute-done.16), channel_id=1, source_target_pairs={{0,1},{1,2},{2,3},{3,4},{4,5},{5,6},{6,7},{8,9},{9,10},{10,11},{11... | collective-permute-start | bytes 786440 | tf_op jit(solution)/shard_map/ppermute | solution.py:18
  198.2 35.9 %collective-permute-start.5 = (bf16[1,128,16,64]{1,3,2,0:T(8,128)(2,1)S(1)}, bf16[1,128,16,64]{1,3,2,0:T(8,128)(2,1)S(1)}, u32[]{:S(2)}, u32[]{:S(2)}) collective-permute-start(bf16[1,128,16,64]{1,3,2,0:T(8,128)(2,1)S(1)} %collective-permute-done.4), channel_id=1, source_target_pairs={{0,1},{1,2},{2,3},{3,4},{4,5},{5,6},{6,7},{8,9},{9,10},{10,11},{11... | collective-permute-start | bytes 786440 | tf_op jit(solution)/shard_map/ppermute | solution.py:18
  210.9 31.3 %collective-permute-start.33 = (bf16[1,128,16,64]{1,3,2,0:T(8,128)(2,1)}, bf16[1,128,16,64]{1,3,2,0:T(8,128)(2,1)}, u32[]{:S(2)}, u32[]{:S(2)}) collective-permute-start(bf16[1,128,16,64]{1,3,2,0:T(8,128)(2,1)} %collective-permute-done.32), channel_id=1, source_target_pairs={{0,1},{1,2},{2,3},{3,4},{4,5},{5,6},{6,7},{8,9},{9,10},{10,11},{11... | collective-permute-start | bytes 786440 | tf_op jit(solution)/shard_map/ppermute | solution.py:18
  216.8 36.7 %collective-permute-start.21 = (bf16[1,128,16,64]{1,3,2,0:T(8,128)(2,1)}, bf16[1,128,16,64]{1,3,2,0:T(8,128)(2,1)}, u32[]{:S(2)}, u32[]{:S(2)}) collective-permute-start(bf16[1,128,16,64]{1,3,2,0:T(8,128)(2,1)} %collective-permute-done.20), channel_id=1, source_target_pairs={{0,1},{1,2},{2,3},{3,4},{4,5},{5,6},{6,7},{8,9},{9,10},{10,11},{11... | collective-permute-start | bytes 786440 | tf_op jit(solution)/shard_map/ppermute | solution.py:18
  220.8 42.7 %collective-permute-start.9 = (bf16[1,128,16,64]{1,3,2,0:T(8,128)(2,1)S(1)}, bf16[1,128,16,64]{1,3,2,0:T(8,128)(2,1)}, u32[]{:S(2)}, u32[]{:S(2)}) collective-permute-start(bf16[1,128,16,64]{1,3,2,0:T(8,128)(2,1)S(1)} %collective-permute-done.8), channel_id=1, source_target_pairs={{0,1},{1,2},{2,3},{3,4},{4,5},{5,6},{6,7},{8,9},{9,10},{10,11},{11... | collective-permute-start | bytes 786440 | tf_op jit(solution)/shard_map/ppermute | solution.py:18
  228.5 46.2 %collective-permute-start.18 = (bf16[1,128,16,64]{1,3,2,0:T(8,128)(2,1)S(1)}, bf16[1,128,16,64]{1,3,2,0:T(8,128)(2,1)}, u32[]{:S(2)}, u32[]{:S(2)}) collective-permute-start(bf16[1,128,16,64]{1,3,2,0:T(8,128)(2,1)S(1)} %collective-permute-done.17), channel_id=1, source_target_pairs={{0,1},{1,2},{2,3},{3,4},{4,5},{5,6},{6,7},{8,9},{9,10},{10,11},{11... | collective-permute-start | bytes 786440 | tf_op jit(solution)/shard_map/ppermute | solution.py:18
  234.1 51.8 %collective-permute-start.6 = (bf16[1,128,16,64]{1,3,2,0:T(8,128)(2,1)S(1)}, bf16[1,128,16,64]{1,3,2,0:T(8,128)(2,1)}, u32[]{:S(2)}, u32[]{:S(2)}) collective-permute-start(bf16[1,128,16,64]{1,3,2,0:T(8,128)(2,1)S(1)} %collective-permute-done.5), channel_id=1, source_target_pairs={{0,1},{1,2},{2,3},{3,4},{4,5},{5,6},{6,7},{8,9},{9,10},{10,11},{11... | collective-permute-start | bytes 786440 | tf_op jit(solution)/shard_map/ppermute | solution.py:18
  242.3 57.3 %collective-permute-start.30 = (bf16[1,128,16,64]{1,3,2,0:T(8,128)(2,1)}, bf16[1,128,16,64]{1,3,2,0:T(8,128)(2,1)}, u32[]{:S(2)}, u32[]{:S(2)}) collective-permute-start(bf16[1,128,16,64]{1,3,2,0:T(8,128)(2,1)} %collective-permute-done.29), channel_id=1, source_target_pairs={{0,1},{1,2},{2,3},{3,4},{4,5},{5,6},{6,7},{8,9},{9,10},{10,11},{11... | collective-permute-start | bytes 786440 | tf_op jit(solution)/shard_map/ppermute | solution.py:18
  253.5 55.3 %collective-permute-start.34 = (bf16[1,128,16,64]{1,3,2,0:T(8,128)(2,1)}, bf16[1,128,16,64]{1,3,2,0:T(8,128)(2,1)}, u32[]{:S(2)}, u32[]{:S(2)}) collective-permute-start(bf16[1,128,16,64]{1,3,2,0:T(8,128)(2,1)} %collective-permute-done.33), channel_id=1, source_target_pairs={{0,1},{1,2},{2,3},{3,4},{4,5},{5,6},{6,7},{8,9},{9,10},{10,11},{11... | collective-permute-start | bytes 786440 | tf_op jit(solution)/shard_map/ppermute | solution.py:18
  263.6 53.9 %collective-permute-start.22 = (bf16[1,128,16,64]{1,3,2,0:T(8,128)(2,1)}, bf16[1,128,16,64]{1,3,2,0:T(8,128)(2,1)}, u32[]{:S(2)}, u32[]{:S(2)}) collective-permute-start(bf16[1,128,16,64]{1,3,2,0:T(8,128)(2,1)} %collective-permute-done.21), channel_id=1, source_target_pairs={{0,1},{1,2},{2,3},{3,4},{4,5},{5,6},{6,7},{8,9},{9,10},{10,11},{11... | collective-permute-start | bytes 786440 | tf_op jit(solution)/shard_map/ppermute | solution.py:18
  274.7 52.6 %collective-permute-start.10 = (bf16[1,128,16,64]{1,3,2,0:T(8,128)(2,1)}, bf16[1,128,16,64]{1,3,2,0:T(8,128)(2,1)}, u32[]{:S(2)}, u32[]{:S(2)}) collective-permute-start(bf16[1,128,16,64]{1,3,2,0:T(8,128)(2,1)} %collective-permute-done.9), channel_id=1, source_target_pairs={{0,1},{1,2},{2,3},{3,4},{4,5},{5,6},{6,7},{8,9},{9,10},{10,11},{11... | collective-permute-start | bytes 786440 | tf_op jit(solution)/shard_map/ppermute | solution.py:18
  285.9 50.2 %collective-permute-start.7 = (bf16[1,128,16,64]{1,3,2,0:T(8,128)(2,1)}, bf16[1,128,16,64]{1,3,2,0:T(8,128)(2,1)}, u32[]{:S(2)}, u32[]{:S(2)}) collective-permute-start(bf16[1,128,16,64]{1,3,2,0:T(8,128)(2,1)} %collective-permute-done.6), channel_id=1, source_target_pairs={{0,1},{1,2},{2,3},{3,4},{4,5},{5,6},{6,7},{8,9},{9,10},{10,11},{11... | collective-permute-start | bytes 786440 | tf_op jit(solution)/shard_map/ppermute | solution.py:18
  300.0 69.6 %collective-permute-start.31 = (bf16[1,128,16,64]{1,3,2,0:T(8,128)(2,1)}, bf16[1,128,16,64]{1,3,2,0:T(8,128)(2,1)}, u32[]{:S(2)}, u32[]{:S(2)}) collective-permute-start(bf16[1,128,16,64]{1,3,2,0:T(8,128)(2,1)} %collective-permute-done.30), channel_id=1, source_target_pairs={{0,1},{1,2},{2,3},{3,4},{4,5},{5,6},{6,7},{8,9},{9,10},{10,11},{11... | collective-permute-start | bytes 786440 | tf_op jit(solution)/shard_map/ppermute | solution.py:18
  308.9 56.3 %collective-permute-start.19 = (bf16[1,128,16,64]{1,3,2,0:T(8,128)(2,1)}, bf16[1,128,16,64]{1,3,2,0:T(8,128)(2,1)}, u32[]{:S(2)}, u32[]{:S(2)}) collective-permute-start(bf16[1,128,16,64]{1,3,2,0:T(8,128)(2,1)} %collective-permute-done.18), channel_id=1, source_target_pairs={{0,1},{1,2},{2,3},{3,4},{4,5},{5,6},{6,7},{8,9},{9,10},{10,11},{11... | collective-permute-start | bytes 786440 | tf_op jit(solution)/shard_map/ppermute | solution.py:18
  317.5 55.7 %collective-permute-start.35 = (bf16[1,128,16,64]{1,3,2,0:T(8,128)(2,1)}, bf16[1,128,16,64]{1,3,2,0:T(8,128)(2,1)}, u32[]{:S(2)}, u32[]{:S(2)}) collective-permute-start(bf16[1,128,16,64]{1,3,2,0:T(8,128)(2,1)} %collective-permute-done.34), channel_id=1, source_target_pairs={{0,1},{1,2},{2,3},{3,4},{4,5},{5,6},{6,7},{8,9},{9,10},{10,11},{11... | collective-permute-start | bytes 786440 | tf_op jit(solution)/shard_map/ppermute | solution.py:18
  327.3 41.4 %collective-permute-start.23 = (bf16[1,128,16,64]{1,3,2,0:T(8,128)(2,1)}, bf16[1,128,16,64]{1,3,2,0:T(8,128)(2,1)}, u32[]{:S(2)}, u32[]{:S(2)}) collective-permute-start(bf16[1,128,16,64]{1,3,2,0:T(8,128)(2,1)} %collective-permute-done.22), channel_id=1, source_target_pairs={{0,1},{1,2},{2,3},{3,4},{4,5},{5,6},{6,7},{8,9},{9,10},{10,11},{11... | collective-permute-start | bytes 786440 | tf_op jit(solution)/shard_map/ppermute | solution.py:18
  336.1 28.2 %collective-permute-start.11 = (bf16[1,128,16,64]{1,3,2,0:T(8,128)(2,1)}, bf16[1,128,16,64]{1,3,2,0:T(8,128)(2,1)}, u32[]{:S(2)}, u32[]{:S(2)}) collective-permute-start(bf16[1,128,16,64]{1,3,2,0:T(8,128)(2,1)} %collective-permute-done.10), channel_id=1, source_target_pairs={{0,1},{1,2},{2,3},{3,4},{4,5},{5,6},{6,7},{8,9},{9,10},{10,11},{11... | collective-permute-start | bytes 786440 | tf_op jit(solution)/shard_map/ppermute | solution.py:18
  666.9 146.8 %collective-permute-start.56 = (bf16[1,128,16,64]{1,3,2,0:T(8,128)(2,1)}, bf16[1,128,16,64]{1,3,2,0:T(8,128)(2,1)}, u32[]{:S(2)}, u32[]{:S(2)}) collective-permute-start(bf16[1,128,16,64]{1,3,2,0:T(8,128)(2,1)} %fusion.499), channel_id=1, source_target_pairs={{0,1},{1,2},{2,3},{3,4},{4,5},{5,6},{6,7},{7,0},{8,9},{9,10},{10,1... | collective-permute-start | bytes 786440 | tf_op jit(solution)/shard_map/ppermute | solution.py:32
  668.4 141.9 %collective-permute-start.61 = (bf16[1,128,16,64]{1,3,2,0:T(8,128)(2,1)}, bf16[1,128,16,64]{1,3,2,0:T(8,128)(2,1)}, u32[]{:S(2)}, u32[]{:S(2)}) collective-permute-start(bf16[1,128,16,64]{1,3,2,0:T(8,128)(2,1)} %fusion.498), channel_id=1, source_target_pairs={{0,1},{1,2},{2,3},{3,4},{4,5},{5,6},{6,7},{7,0},{8,9},{9,10},{10,1... | collective-permute-start | bytes 786440 | tf_op jit(solution)/shard_map/ppermute | solution.py:32
  676.5 143.0 %collective-permute-start.46 = (bf16[1,128,16,64]{1,3,2,0:T(8,128)(2,1)}, bf16[1,128,16,64]{1,3,2,0:T(8,128)(2,1)}, u32[]{:S(2)}, u32[]{:S(2)}) collective-permute-start(bf16[1,128,16,64]{1,3,2,0:T(8,128)(2,1)} %fusion.500), channel_id=1, source_target_pairs={{0,1},{1,2},{2,3},{3,4},{4,5},{5,6},{6,7},{7,0},{8,9},{9,10},{10,1... | collective-permute-start | bytes 786440 | tf_op jit(solution)/shard_map/ppermute | solution.py:32
  681.5 134.6 %collective-permute-start.51 = (bf16[1,128,16,64]{1,3,2,0:T(8,128)(2,1)}, bf16[1,128,16,64]{1,3,2,0:T(8,128)(2,1)}, u32[]{:S(2)}, u32[]{:S(2)}) collective-permute-start(bf16[1,128,16,64]{1,3,2,0:T(8,128)(2,1)} %fusion.497), channel_id=1, source_target_pairs={{0,1},{1,2},{2,3},{3,4},{4,5},{5,6},{6,7},{7,0},{8,9},{9,10},{10,1... | collective-permute-start | bytes 786440 | tf_op jit(solution)/shard_map/ppermute | solution.py:32
  700.6 123.1 %collective-permute-start.36 = (bf16[1,128,16,64]{1,3,2,0:T(8,128)(2,1)}, bf16[1,128,16,64]{1,3,2,0:T(8,128)(2,1)}, u32[]{:S(2)}, u32[]{:S(2)}) collective-permute-start(bf16[1,128,16,64]{1,3,2,0:T(8,128)(2,1)} %fusion.501), channel_id=1, source_target_pairs={{0,1},{1,2},{2,3},{3,4},{4,5},{5,6},{6,7},{7,0},{8,9},{9,10},{10,1... | collective-permute-start | bytes 786440 | tf_op jit(solution)/shard_map/ppermute | solution.py:32
  823.7 30.0 %collective-permute-start.42 = (bf16[1,128,16,64]{1,3,2,0:T(8,128)(2,1)S(1)}, bf16[1,128,16,64]{1,3,2,0:T(8,128)(2,1)S(1)}, u32[]{:S(2)}, u32[]{:S(2)}) collective-permute-start(bf16[1,128,16,64]{1,3,2,0:T(8,128)(2,1)S(1)} %add_convert_fusion.22), channel_id=1, source_target_pairs={{0,1},{1,2},{2,3},{3,4},{4,5},{5,6},{6,7},{7,0},{8,9},{9,10},{10,1... | collective-permute-start | bytes 786440 | tf_op jit(solution)/shard_map/ppermute | solution.py:32
  830.6 28.7 %collective-permute-start.37 = (bf16[1,128,16,64]{1,3,2,0:T(8,128)(2,1)S(1)}, bf16[1,128,16,64]{1,3,2,0:T(8,128)(2,1)S(1)}, u32[]{:S(2)}, u32[]{:S(2)}) collective-permute-start(bf16[1,128,16,64]{1,3,2,0:T(8,128)(2,1)S(1)} %add_convert_fusion.26), channel_id=1, source_target_pairs={{0,1},{1,2},{2,3},{3,4},{4,5},{5,6},{6,7},{7,0},{8,9},{9,10},{10,1... | collective-permute-start | bytes 786440 | tf_op jit(solution)/shard_map/ppermute | solution.py:32
  836.9 28.1 %collective-permute-start.63 = (bf16[1,128,16,64]{1,3,2,0:T(8,128)(2,1)S(1)}, bf16[1,128,16,64]{1,3,2,0:T(8,128)(2,1)S(1)}, u32[]{:S(2)}, u32[]{:S(2)}) collective-permute-start(bf16[1,128,16,64]{1,3,2,0:T(8,128)(2,1)S(1)} %add_convert_fusion.3), channel_id=1, source_target_pairs={{0,1},{1,2},{2,3},{3,4},{4,5},{5,6},{6,7},{7,0},{8,9},{9,10},{10,1... | collective-permute-start | bytes 786440 | tf_op jit(solution)/shard_map/ppermute | solution.py:32
  842.5 28.1 %collective-permute-start.58 = (bf16[1,128,16,64]{1,3,2,0:T(8,128)(2,1)S(1)}, bf16[1,128,16,64]{1,3,2,0:T(8,128)(2,1)S(1)}, u32[]{:S(2)}, u32[]{:S(2)}) collective-permute-start(bf16[1,128,16,64]{1,3,2,0:T(8,128)(2,1)S(1)} %add_convert_fusion.7), channel_id=1, source_target_pairs={{0,1},{1,2},{2,3},{3,4},{4,5},{5,6},{6,7},{7,0},{8,9},{9,10},{10,1... | collective-permute-start | bytes 786440 | tf_op jit(solution)/shard_map/ppermute | solution.py:32
  848.1 28.1 %collective-permute-start.53 = (bf16[1,128,16,64]{1,3,2,0:T(8,128)(2,1)S(1)}, bf16[1,128,16,64]{1,3,2,0:T(8,128)(2,1)S(1)}, u32[]{:S(2)}, u32[]{:S(2)}) collective-permute-start(bf16[1,128,16,64]{1,3,2,0:T(8,128)(2,1)S(1)} %add_convert_fusion.12), channel_id=1, source_target_pairs={{0,1},{1,2},{2,3},{3,4},{4,5},{5,6},{6,7},{7,0},{8,9},{9,10},{10,1... | collective-permute-start | bytes 786440 | tf_op jit(solution)/shard_map/ppermute | solution.py:32
  853.7 28.1 %collective-permute-start.48 = (bf16[1,128,16,64]{1,3,2,0:T(8,128)(2,1)S(1)}, bf16[1,128,16,64]{1,3,2,0:T(8,128)(2,1)S(1)}, u32[]{:S(2)}, u32[]{:S(2)}) collective-permute-start(bf16[1,128,16,64]{1,3,2,0:T(8,128)(2,1)S(1)} %add_convert_fusion.16), channel_id=1, source_target_pairs={{0,1},{1,2},{2,3},{3,4},{4,5},{5,6},{6,7},{7,0},{8,9},{9,10},{10,1... | collective-permute-start | bytes 786440 | tf_op jit(solution)/shard_map/ppermute | solution.py:32
  859.3 28.1 %collective-permute-start.43 = (bf16[1,128,16,64]{1,3,2,0:T(8,128)(2,1)S(1)}, bf16[1,128,16,64]{1,3,2,0:T(8,128)(2,1)S(1)}, u32[]{:S(2)}, u32[]{:S(2)}) collective-permute-start(bf16[1,128,16,64]{1,3,2,0:T(8,128)(2,1)S(1)} %add_convert_fusion.21), channel_id=1, source_target_pairs={{0,1},{1,2},{2,3},{3,4},{4,5},{5,6},{6,7},{7,0},{8,9},{9,10},{10,1... | collective-permute-start | bytes 786440 | tf_op jit(solution)/shard_map/ppermute | solution.py:32
  864.9 28.1 %collective-permute-start.38 = (bf16[1,128,16,64]{1,3,2,0:T(8,128)(2,1)S(1)}, bf16[1,128,16,64]{1,3,2,0:T(8,128)(2,1)S(1)}, u32[]{:S(2)}, u32[]{:S(2)}) collective-permute-start(bf16[1,128,16,64]{1,3,2,0:T(8,128)(2,1)S(1)} %add_convert_fusion.25), channel_id=1, source_target_pairs={{0,1},{1,2},{2,3},{3,4},{4,5},{5,6},{6,7},{7,0},{8,9},{9,10},{10,1... | collective-permute-start | bytes 786440 | tf_op jit(solution)/shard_map/ppermute | solution.py:32
  870.6 34.0 %collective-permute-start.64 = (bf16[1,128,16,64]{1,3,2,0:T(8,128)(2,1)S(1)}, bf16[1,128,16,64]{1,3,2,0:T(8,128)(2,1)S(1)}, u32[]{:S(2)}, u32[]{:S(2)}) collective-permute-start(bf16[1,128,16,64]{1,3,2,0:T(8,128)(2,1)S(1)} %add_convert_fusion.2), channel_id=1, source_target_pairs={{0,1},{1,2},{2,3},{3,4},{4,5},{5,6},{6,7},{7,0},{8,9},{9,10},{10,1... | collective-permute-start | bytes 786440 | tf_op jit(solution)/shard_map/ppermute | solution.py:32
  876.2 28.1 %collective-permute-start.59 = (bf16[1,128,16,64]{1,3,2,0:T(8,128)(2,1)S(1)}, bf16[1,128,16,64]{1,3,2,0:T(8,128)(2,1)S(1)}, u32[]{:S(2)}, u32[]{:S(2)}) collective-permute-start(bf16[1,128,16,64]{1,3,2,0:T(8,128)(2,1)S(1)} %add_convert_fusion.6), channel_id=1, source_target_pairs={{0,1},{1,2},{2,3},{3,4},{4,5},{5,6},{6,7},{7,0},{8,9},{9,10},{10,1... | collective-permute-start | bytes 786440 | tf_op jit(solution)/shard_map/ppermute | solution.py:32
  881.8 35.9 %collective-permute-start.54 = (bf16[1,128,16,64]{1,3,2,0:T(8,128)(2,1)S(1)}, bf16[1,128,16,64]{1,3,2,0:T(8,128)(2,1)S(1)}, u32[]{:S(2)}, u32[]{:S(2)}) collective-permute-start(bf16[1,128,16,64]{1,3,2,0:T(8,128)(2,1)S(1)} %add_convert_fusion.11), channel_id=1, source_target_pairs={{0,1},{1,2},{2,3},{3,4},{4,5},{5,6},{6,7},{7,0},{8,9},{9,10},{10,1... | collective-permute-start | bytes 786440 | tf_op jit(solution)/shard_map/ppermute | solution.py:32
  887.4 28.1 %collective-permute-start.49 = (bf16[1,128,16,64]{1,3,2,0:T(8,128)(2,1)S(1)}, bf16[1,128,16,64]{1,3,2,0:T(8,128)(2,1)S(1)}, u32[]{:S(2)}, u32[]{:S(2)}) collective-permute-start(bf16[1,128,16,64]{1,3,2,0:T(8,128)(2,1)S(1)} %add_convert_fusion.15), channel_id=1, source_target_pairs={{0,1},{1,2},{2,3},{3,4},{4,5},{5,6},{6,7},{7,0},{8,9},{9,10},{10,1... | collective-permute-start | bytes 786440 | tf_op jit(solution)/shard_map/ppermute | solution.py:32
  904.6 51.4 %collective-permute-start.60 = (bf16[1,128,16,64]{1,3,2,0:T(8,128)(2,1)S(1)}, bf16[1,128,16,64]{1,3,2,0:T(8,128)(2,1)S(1)}, u32[]{:S(2)}, u32[]{:S(2)}) collective-permute-start(bf16[1,128,16,64]{1,3,2,0:T(8,128)(2,1)S(1)} %add_convert_fusion.5), channel_id=1, source_target_pairs={{0,4},{1,5},{2,6},{3,7},{4,0},{5,1},{6,2},{7,3},{8,12},{9,13},{10,... | collective-permute-start | bytes 786440 | tf_op jit(solution)/shard_map/ppermute | solution.py:32
  915.5 40.6 %collective-permute-start.65 = (bf16[1,128,16,64]{1,3,2,0:T(8,128)(2,1)S(1)}, bf16[1,128,16,64]{1,3,2,0:T(8,128)(2,1)S(1)}, u32[]{:S(2)}, u32[]{:S(2)}) collective-permute-start(bf16[1,128,16,64]{1,3,2,0:T(8,128)(2,1)S(1)} %add_convert_fusion.1), channel_id=1, source_target_pairs={{0,4},{1,5},{2,6},{3,7},{4,0},{5,1},{6,2},{7,3},{8,12},{9,13},{10,... | collective-permute-start | bytes 786440 | tf_op jit(solution)/shard_map/ppermute | solution.py:32
  917.8 43.6 %collective-permute-start.50 = (bf16[1,128,16,64]{1,3,2,0:T(8,128)(2,1)S(1)}, bf16[1,128,16,64]{1,3,2,0:T(8,128)(2,1)S(1)}, u32[]{:S(2)}, u32[]{:S(2)}) collective-permute-start(bf16[1,128,16,64]{1,3,2,0:T(8,128)(2,1)S(1)} %add_convert_fusion.14), channel_id=1, source_target_pairs={{0,4},{1,5},{2,6},{3,7},{4,0},{5,1},{6,2},{7,3},{8,12},{9,13},{10,... | collective-permute-start | bytes 786440 | tf_op jit(solution)/shard_map/ppermute | solution.py:32
  921.1 42.3 %collective-permute-start.55 = (bf16[1,128,16,64]{1,3,2,0:T(8,128)(2,1)S(1)}, bf16[1,128,16,64]{1,3,2,0:T(8,128)(2,1)S(1)}, u32[]{:S(2)}, u32[]{:S(2)}) collective-permute-start(bf16[1,128,16,64]{1,3,2,0:T(8,128)(2,1)S(1)} %add_convert_fusion.10), channel_id=1, source_target_pairs={{0,4},{1,5},{2,6},{3,7},{4,0},{5,1},{6,2},{7,3},{8,12},{9,13},{10,... | collective-permute-start | bytes 786440 | tf_op jit(solution)/shard_map/ppermute | solution.py:32
  926.7 43.3 %collective-permute-start.45 = (bf16[1,128,16,64]{1,3,2,0:T(8,128)(2,1)S(1)}, bf16[1,128,16,64]{1,3,2,0:T(8,128)(2,1)S(1)}, u32[]{:S(2)}, u32[]{:S(2)}) collective-permute-start(bf16[1,128,16,64]{1,3,2,0:T(8,128)(2,1)S(1)} %add_convert_fusion.19), channel_id=1, source_target_pairs={{0,4},{1,5},{2,6},{3,7},{4,0},{5,1},{6,2},{7,3},{8,12},{9,13},{10,... | collective-permute-start | bytes 786440 | tf_op jit(solution)/shard_map/ppermute | solution.py:32
  (269 other events, 5681.5 us)
Sparse Core Ops, SparseCore 0:
  9.6 20.8 all-gather.10
  32.0 16.7 all-gather.14
  50.8 99.9 all-gather.6
  152.7 64.6 all-gather.8
  219.4 205.5 all-gather.12
  426.9 123.1 all-gather.16
  726.3 330.2 all-reduce.3
where the time goes:
time: 1080 us; the launch traced here: 1070 us
  waiting for transfers between devices  416 us (39%)
  starting transfers between devices  275 us (25%)
  matrix products  174 us (16%)
  blocking collectives  87.4 us (8%)
  local copies, waits for them, and re-layouts  52 us (5%)
  other arithmetic  33.4 us (3%)
  between operations  26.1 us (2%)
    ppermute x36, starting transfers between devices, passed_along(): lax.ppermute(value, axis, [(source, source + steps) for source in range(i...  204 us
    all_gather x1, waiting for transfers between devices, local(): lax.all_gather(lax.all_gather(proj_weight, 'row', axis=0, tiled=True), 's...  119 us
    ppermute x30, waiting for transfers between devices, shifted(): return lax.ppermute(value, axis, pairs)  105 us
    psum x1, waiting for transfers between devices, local(): lax.psum((local_grads[0], local_grads[1], local_grads[2], local_grads[3],...  74.8 us
    ppermute x30, starting transfers between devices, shifted(): return lax.ppermute(value, axis, pairs)  70.8 us
    psum x1, blocking collectives, local(): lax.psum((local_grads[0], local_grads[1], local_grads[2], local_grads[3],...  67.4 us
    dot_general x9, matrix products, dot_transposed(): lax.dot_general(left_op, right_op, (((1,), (1,)), ((), ())), preferred_el...  61.4 us
    all_gather x1, waiting for transfers between devices, local(): lax.all_gather(lax.all_gather(fc_weight, 'row', axis=0, tiled=True), 'seq...  43.3 us
  transfers between devices with their start and end apart: 73, of which 27 were waited for; matrix products, arithmetic and copies ran while one was open for 11% of the time, Pallas kernels for 0%

commit v1 on v0

v1 whole, which is shorter than its diff:
```python
import math

import jax
import jax.numpy as jnp
import numpy as np
from jax import lax
from jax.experimental import pallas as pl
from jax.experimental.pallas import tpu as pltpu
from jax.sharding import PartitionSpec as P

HEADS = 16
SEG_MOST = 512
EPS = 1e-05
MASKED = -1e30
BF = jnp.bfloat16
F32 = jnp.float32
MIB = 1 << 20

VMEM = pltpu.VMEM


def mm(left, right):
    return jnp.dot(left, right, preferred_element_type=F32)


def mm_nt(left, right):
    return lax.dot_general(left, right, (((1,), (1,)), ((), ())), preferred_element_type=F32)


def mm_tn(left, right):
    return lax.dot_general(left, right, (((0,), (0,)), ((), ())), preferred_element_type=F32)


def matmul_high(left_op, right_op):
    return jnp.dot(
        left_op, right_op, precision=lax.Precision.HIGHEST, preferred_element_type=F32
    )


def swapped(value, axis, bit):
    count = lax.axis_size(axis)
    return lax.ppermute(value, axis, [(i, i ^ bit) for i in range(count)])


def moved(value, axis, steps):
    count = lax.axis_size(axis)
    low, high = max(0, -steps), min(count, count - steps)
    return lax.ppermute(value, axis, [(i, i + steps) for i in range(low, high)])


def summed_all(value):
    for axis in ("row", "seq"):
        bit = 1
        while bit < lax.axis_size(axis):
            value = value + swapped(value, axis, bit)
            bit *= 2
    return value


def cat(*parts):
    return jnp.concatenate(parts, axis=0)


X, ZN, ZF, CORE, Y = ("seq", 1), ("seq", 2), ("seq", 4), ("row", 1), ("row", 2)


def plane(block, first, second):
    half = cat(block, swapped(block, *first))
    whole = cat(half, swapped(half, *second))
    return cat(whole, swapped(whole, *CORE))


def gathered(shard, order):
    near = cat(shard, swapped(shard, *ZF))
    across = swapped(near, *ZN)
    return cat(plane(near, *order), plane(across, *order))


def piece_table(x_first):
    rel_row = jnp.arange(4, dtype=jnp.int32)[:, None] ^ lax.axis_index("row")
    rel_seq = jnp.arange(8, dtype=jnp.int32)[None, :] ^ lax.axis_index("seq")
    far, near, across_x = (rel_seq >> 2) & 1, (rel_seq >> 1) & 1, rel_seq & 1
    across_y, core = (rel_row >> 1) & 1, rel_row & 1
    one, two = (across_x, across_y) if x_first else (across_y, across_x)
    return (far | (one << 1) | (two << 2) | (core << 3) | (near << 4)).reshape(32)


def norm_parts(values):
    centre = values - jnp.mean(values, axis=-1, keepdims=True)
    spread = jnp.mean(centre * centre, axis=-1, keepdims=True)
    scale = lax.rsqrt(spread + EPS)
    return centre * scale, scale


def norm_back(values, incoming, gain):
    normal, scale = norm_parts(values)
    e = incoming * gain
    return scale * (
        e
        - jnp.mean(e, axis=-1, keepdims=True)
        - normal * jnp.mean(e * normal, axis=-1, keepdims=True)
    )


def params(limit, semantics=None):
    return pltpu.CompilerParams(vmem_limit_bytes=limit * MIB, dimension_semantics=semantics)


def whole(shape):
    return pl.BlockSpec(shape, lambda *_: (0,) * len(shape))


def piece(rows, cols, where):
    return pl.BlockSpec((1, rows, cols), where)


def qkv_kernel(tab, own, o1, h1, r2, h2, w0, w1, w2, w3, bias, mixed, natural, wide):
    step = pl.program_id(0)
    tokens = own.shape[0]
    for r, w in enumerate((w0, w1, w2, w3)):
        wide[256 * r : 256 * (r + 1), :] = w[0, :, :384]
    natural[...] = wide[...]

    def one(slot, block):
        value = (mm(block, wide[...]) + bias[...].astype(F32)).astype(BF)
        for col in range(3):
            mixed[col, slot] = value[:, 128 * col : 128 * (col + 1)]

    one(0, own[...])

    @pl.when(step >= 2)
    def _():
        for slot, ref in enumerate((o1, h1, r2, h2)):
            one(slot + 1, ref[:tokens, :])


def qkv_call(table, blocks, weights, bias, tokens, width):
    halo_rows = blocks[1].shape[0]
    return pl.pallas_call(
        qkv_kernel,
        grid_spec=pltpu.PrefetchScalarGridSpec(
            num_scalar_prefetch=1,
            grid=(8,),
            in_specs=[whole((tokens, width))]
            + [whole((halo_rows, width))] * 4
            + [
                piece(256, 512, lambda s, tab, r=r: (tab[r * 8 + s], 0, 0))
                for r in range(4)
            ]
            + [pl.BlockSpec((1, 384), lambda s, tab: (0, s))],
            out_specs=[
                pl.BlockSpec((3, 5, tokens, 128), lambda s, tab: (s, 0, 0, 0)),
                pl.BlockSpec((1024, 384), lambda s, tab: (0, s)),
            ],
            scratch_shapes=[VMEM((1024, 384), BF)],
        ),
        out_shape=[
            jax.ShapeDtypeStruct((24, 5, tokens, 128), BF),
            jax.ShapeDtypeStruct((1024, 3072), BF),
        ],
        compiler_params=params(32),
        cost_estimate=pl.CostEstimate(
            flops=2 * tokens * 1024 * 1024 * 11, bytes_accessed=20 * MIB, transcendentals=0
        ),
        name="qkv",
    )(table, *blocks, weights, weights, weights, weights, bias)


def allowed_bias(seg, out):
    query = jnp.broadcast_to(seg[0:1, :], (128, 128))
    key_at = lax.broadcasted_iota(jnp.int32, (128, 128), 0)
    query_at = lax.broadcasted_iota(jnp.int32, (128, 128), 1)
    out[0:128, :] = jnp.where(key_at < 10, 0.0, MASKED)
    for slot in range(5):
        key = jnp.broadcast_to(seg[slot : slot + 1, :], (128, 128)).T
        allowed = key == query
        if slot == 0:
            allowed = allowed & (key_at <= query_at)
        out[128 * (slot + 1) : 128 * (slot + 2), :] = jnp.where(allowed, 0.0, MASKED)


def two_heads(block):
    lane = lax.broadcasted_iota(jnp.int32, block.shape, 1)
    zero = jnp.zeros_like(block)
    return cat(jnp.where(lane < 64, block, zero), jnp.where(lane < 64, zero, block))


def heads_merged(both):
    feature = lax.broadcasted_iota(jnp.int32, (128, 128), 0)
    return jnp.where(feature < 64, both[:, :128], both[:, 128:]).T


def attend_kernel(seg, q, k, v, pk, pv, att, probs, bias):
    allowed_bias(seg[0], bias)

    def pair(p, carry):
        keys = cat(pk[p], *[k[p, slot] for slot in range(5)])
        values = cat(pv[p], *[v[p, slot] for slot in range(5)])
        queries = two_heads(q[p, 0] * 0.125)
        scores = mm_nt(keys, queries) + jnp.concatenate([bias[...], bias[...]], axis=1)
        top = jnp.max(scores, axis=0, keepdims=True)
        expo = jnp.exp(scores - top)
        total = jnp.sum(expo, axis=0, keepdims=True)
        chance = (expo * (1.0 / total)).astype(BF)
        probs[0, p] = chance
        att[:, pl.ds(pl.multiple_of(p * 128, 128), 128)] = heads_merged(
            mm_tn(values, chance)
        ).astype(BF)
        return carry

    lax.fori_loop(0, 8, pair, 0)


def attend_call(seg, mixed, pk, pv, batches, tokens):
    return pl.pallas_call(
        attend_kernel,
        grid=(batches,),
        in_specs=[
            pl.BlockSpec((1, 5, 128), lambda b: (b, 0, 0)),
            pl.BlockSpec((8, 1, 128, 128), lambda b: (0, 0, b, 0)),
            pl.BlockSpec((8, 5, 128, 128), lambda b: (1, 0, b, 0)),
            pl.BlockSpec((8, 5, 128, 128), lambda b: (2, 0, b, 0)),
            whole((8, 128, 128)),
            whole((8, 128, 128)),
        ],
        out_specs=[
            pl.BlockSpec((128, 1024), lambda b: (b, 0)),
            pl.BlockSpec((1, 8, 768, 256), lambda b: (b, 0, 0, 0)),
        ],
        out_shape=[
            jax.ShapeDtypeStruct((tokens, 1024), BF),
            jax.ShapeDtypeStruct((batches, 8, 768, 256), BF),
        ],
        scratch_shapes=[VMEM((768, 128), F32)],
        compiler_params=params(32),
        cost_estimate=pl.CostEstimate(
            flops=24 * 2 * 2 * 768 * 256 * 256,
            bytes_accessed=20 * MIB,
            transcendentals=24 * 768 * 256,
        ),
        name="attend",
    )(seg, mixed, mixed, mixed, pk, pv)


def middle_kernel(tab, att, x, *refs):
    ws, (out_bias, gain, shift, middle, normed, natural, wide, total) = refs[:8], refs[8:]
    step = pl.program_id(0)
    for r in range(4):
        for half in range(2):
            wide[256 * r : 256 * (r + 1), 128 * half : 128 * (half + 1)] = ws[2 * r + half][0]
    natural[...] = wide[...]
    cols = pl.ds(pl.multiple_of(step * 256, 256), 256)
    total[:, cols] = mm(att[...], wide[...])

    @pl.when(step == 3)
    def _():
        value = x[...].astype(F32) + total[...] + out_bias[...].astype(F32)
        middle[...] = value
        normal, _ = norm_parts(value)
        normed[...] = (normal * gain[...].astype(F32) + shift[...].astype(F32)).astype(BF)


def middle_call(table, att, x, weights, out_bias, gain, shift, tokens):
    return pl.pallas_call(
        middle_kernel,
        grid_spec=pltpu.PrefetchScalarGridSpec(
            num_scalar_prefetch=1,
            grid=(4,),
            in_specs=[whole((tokens, 1024))] * 2
            + [
                piece(256, 128, lambda i, tab, r=r, h=h: (tab[r * 8 + 2 * i + h], 0, 3))
                for r in range(4)
                for h in range(2)
            ]
            + [whole((1, 1024))] * 3,
            out_specs=[
                whole((tokens, 1024)),
                whole((tokens, 1024)),
                pl.BlockSpec((1024, 256), lambda i, tab: (0, i)),
            ],
            scratch_shapes=[VMEM((1024, 256), BF), VMEM((tokens, 1024), F32)],
        ),
        out_shape=[
            jax.ShapeDtypeStruct((tokens, 1024), F32),
            jax.ShapeDtypeStruct((tokens, 1024), BF),
            jax.ShapeDtypeStruct((1024, 1024), BF),
        ],
        compiler_params=params(24),
        cost_estimate=pl.CostEstimate(
            flops=2 * tokens * 1024 * 1024, bytes_accessed=8 * MIB, transcendentals=0
        ),
        name="middle",
    )(table, att, x, *[weights] * 8, out_bias, gain, shift)


def hidden_kernel(tab, normed, w0, w1, w2, w3, bias, hidden, slope, wide):
    for r, w in enumerate((w0, w1, w2, w3)):
        wide[256 * r : 256 * (r + 1), :] = w[0]
    v = mm(normed[...], wide[...]) + bias[...].astype(F32)
    square = v * v
    inner = 0.7978845608028654 * v * (1.0 + 0.044715 * square)
    t = jnp.tanh(inner)
    hidden[...] = (0.5 * v * (1.0 + t)).astype(BF)
    slope[...] = (
        0.5 * (1.0 + t)
        + 0.5 * v * (1.0 - t * t) * (0.7978845608028654 * (1.0 + 3 * 0.044715 * square))
    ).astype(BF)


def hidden_call(table, normed, weights, bias, tokens):
    return pl.pallas_call(
        hidden_kernel,
        grid_spec=pltpu.PrefetchScalarGridSpec(
            num_scalar_prefetch=1,
            grid=(8,),
            in_specs=[whole((tokens, 1024))]
            + [
                piece(256, 512, lambda s, tab, r=r: (tab[r * 8 + s], 0, 0))
                for r in range(4)
            ]
            + [pl.BlockSpec((1, 512), lambda s, tab: (0, s))],
            out_specs=[
                pl.BlockSpec((tokens, 512), lambda s, tab: (0, s)),
                pl.BlockSpec((tokens, 512), lambda s, tab: (0, s)),
            ],
            scratch_shapes=[VMEM((1024, 512), BF)],
        ),
        out_shape=[jax.ShapeDtypeStruct((tokens, 4096), BF)] * 2,
        compiler_params=params(24),
        cost_estimate=pl.CostEstimate(
            flops=2 * tokens * 1024 * 4096,
            bytes_accessed=16 * MIB,
            transcendentals=tokens * 4096,
        ),
        name="hidden",
    )(table, normed, *[weights] * 4, bias)


def grad_pre_kernel(tab, cot, *refs):
    ws, (slope, grad_pre, natural) = refs[:8], refs[8:]
    for s in range(8):
        for j in range(4):
            natural[256 * j : 256 * (j + 1), 128 * s : 128 * (s + 1)] = ws[s][
                0, :, 128 * j : 128 * (j + 1)
            ]
    grad_hidden = mm_nt(cot[...], natural[...])
    grad_pre[...] = (grad_hidden * slope[...].astype(F32)).astype(BF)


def grad_pre_call(table, cot, weights, slope, tokens):
    return pl.pallas_call(
        grad_pre_kernel,
        grid_spec=pltpu.PrefetchScalarGridSpec(
            num_scalar_prefetch=1,
            grid=(4,),
            in_specs=[whole((tokens, 1024))]
            + [
                piece(256, 512, lambda r, tab, s=s: (tab[r * 8 + s], 0, 0))
                for s in range(8)
            ]
            + [pl.BlockSpec((tokens, 1024), lambda r, tab: (0, r))],
            out_specs=[
                pl.BlockSpec((tokens, 1024), lambda r, tab: (0, r)),
                pl.BlockSpec((1024, 1024), lambda r, tab: (r, 0)),
            ],
        ),
        out_shape=[
            jax.ShapeDtypeStruct((tokens, 4096), BF),
            jax.ShapeDtypeStruct((4096, 1024), BF),
        ],
        compiler_params=params(24),
        cost_estimate=pl.CostEstimate(
            flops=2 * tokens * 1024 * 4096, bytes_accessed=16 * MIB, transcendentals=0
        ),
        name="grad_pre",
    )(table, cot, *[weights] * 8, slope)


def grad_middle_kernel(
    tab, grad_pre, w0, w1, w2, w3, cot, middle, gain, out_nat, grad_mid, grad_att, wide, total
):
    step = pl.program_id(0)
    for r, w in enumerate((w0, w1, w2, w3)):
        wide[256 * r : 256 * (r + 1), :] = w[0]
    part = mm_nt(grad_pre[...], wide[...])

    @pl.when(step == 0)
    def _():
        total[...] = part

    @pl.when(step > 0)
    def _():
        total[...] += part

    @pl.when(step == 7)
    def _():
        value = cot[...].astype(F32) + norm_back(middle[...], total[...], gain[...].astype(F32))
        grad_mid[...] = value
        grad_att[...] = mm_nt(value.astype(BF), out_nat[...]).astype(BF)


def grad_middle_call(table, grad_pre, weights, cot, middle, gain, out_nat, tokens):
    return pl.pallas_call(
        grad_middle_kernel,
        grid_spec=pltpu.PrefetchScalarGridSpec(
            num_scalar_prefetch=1,
            grid=(8,),
            in_specs=[pl.BlockSpec((tokens, 512), lambda s, tab: (0, s))]
            + [
                piece(256, 512, lambda s, tab, r=r: (tab[r * 8 + s], 0, 0))
                for r in range(4)
            ]
            + [
                whole((tokens, 1024)),
                whole((tokens, 1024)),
                whole((1, 1024)),
                whole((1024, 1024)),
            ],
            out_specs=[whole((tokens, 1024)), whole((tokens, 1024))],
            scratch_shapes=[VMEM((1024, 512), BF), VMEM((tokens, 1024), F32)],
        ),
        out_shape=[
            jax.ShapeDtypeStruct((tokens, 1024), F32),
            jax.ShapeDtypeStruct((tokens, 1024), BF),
        ],
        compiler_params=params(32),
        cost_estimate=pl.CostEstimate(
            flops=2 * tokens * 1024 * 5120, bytes_accessed=16 * MIB, transcendentals=0
        ),
        name="grad_middle",
    )(table, grad_pre, *[weights] * 4, cot, middle, gain, out_nat)


def attend_back_kernel(
    q, k, v, pk, pv, probs, grad_att, att, w_nat, side, near, far, own, grad_pre_kv, dkv
):
    ones = jnp.ones((8, 128), F32)
    lane = lax.broadcasted_iota(jnp.int32, (8, 128), 1)

    def pair(p, carry):
        cols = pl.ds(pl.multiple_of(p * 128, 128), 128)
        cols_v = pl.ds(pl.multiple_of(p * 128 + 1024, 128), 128)
        keys = cat(pk[p], *[k[p, slot] for slot in range(5)])
        values = cat(pv[p], *[v[p, slot] for slot in range(5)])
        queries = two_heads(q[p, 0] * 0.125)
        grad_o = grad_att[:, cols]
        grad_two = two_heads(grad_o)
        product = grad_o.astype(F32) * att[:, cols].astype(F32)
        prec = lax.Precision.HIGHEST
        delta = jnp.concatenate(
            [
                lax.dot_general(
                    jnp.where((lane < 64) == first, ones, 0.0),
                    product,
                    (((1,), (1,)), ((), ())),
                    precision=prec,
                    preferred_element_type=F32,
                )[0:1, :]
                for first in (True, False)
            ],
            axis=1,
        )
        chance = probs[0, p]
        grad_probs = mm_nt(values, grad_two)
        grad_scores = (chance.astype(F32) * (grad_probs - delta)).astype(BF)
        grad_k = mm(grad_scores, queries)
        grad_v = mm(chance, grad_two)
        grad_q = heads_merged(mm_tn(keys, grad_scores)) * 0.125
        own[:, cols] = grad_q.astype(BF)
        grad_pre_kv[0, p] = grad_k[:16]
        grad_pre_kv[1, p] = grad_v[:16]
        for slot in range(5):
            rows = slice(128 * (slot + 1), 128 * (slot + 2))
            if slot == 0:
                own[:, pl.ds(pl.multiple_of(p * 128 + 1024, 128), 128)] = grad_k[rows].astype(BF)
                own[:, pl.ds(pl.multiple_of(p * 128 + 2048, 128), 128)] = grad_v[rows].astype(BF)
            else:
                dkv[slot - 1, :, cols] = grad_k[rows].astype(BF)
                dkv[slot - 1, :, cols_v] = grad_v[rows].astype(BF)
        return carry

    lax.fori_loop(0, 8, pair, 0)
    w_kv = w_nat[:, 1024:]
    side[0] = mm_nt(dkv[0], w_kv).astype(BF)
    side[1] = mm_nt(dkv[2], w_kv).astype(BF)
    near[...] = mm_nt(dkv[1], w_kv).astype(BF)
    far[...] = mm_nt(dkv[3], w_kv).astype(BF)


def attend_back_call(batch, mixed, pk, pv, probs, grad_att, att, w_nat):
    return pl.pallas_call(
        attend_back_kernel,
        grid=(1,),
        in_specs=[
            pl.BlockSpec((8, 1, 128, 128), lambda b: (0, 0, batch, 0)),
            pl.BlockSpec((8, 5, 128, 128), lambda b: (1, 0, batch, 0)),
            pl.BlockSpec((8, 5, 128, 128), lambda b: (2, 0, batch, 0)),
            whole((8, 128, 128)),
            whole((8, 128, 128)),
            pl.BlockSpec((1, 8, 768, 256), lambda b: (batch, 0, 0, 0)),
            pl.BlockSpec((128, 1024), lambda b: (batch, 0)),
            pl.BlockSpec((128, 1024), lambda b: (batch, 0)),
            whole((1024, 3072)),
        ],
        out_specs=[
            whole((2, 128, 1024)),
            whole((128, 1024)),
            whole((128, 1024)),
            whole((128, 3072)),
            whole((2, 8, 16, 128)),
        ],
        out_shape=[
            jax.ShapeDtypeStruct((2, 128, 1024), BF),
            jax.ShapeDtypeStruct((128, 1024), BF),
            jax.ShapeDtypeStruct((128, 1024), BF),
            jax.ShapeDtypeStruct((128, 3072), BF),
            jax.ShapeDtypeStruct((2, 8, 16, 128), F32),
        ],
        scratch_shapes=[VMEM((4, 128, 2048), BF)],
        compiler_params=params(40),
        cost_estimate=pl.CostEstimate(
            flops=8 * 4 * 2 * 768 * 256 * 256 + 2 * 512 * 2048 * 1024,
            bytes_accessed=16 * MIB,
            transcendentals=0,
        ),
        name="attend_back",
    )(mixed, mixed, mixed, pk, pv, probs, grad_att, att, w_nat)


def units_gathered(qkv_weight, out_weight, fc_weight, proj_weight):
    row_count, seq_count = lax.axis_size("row"), lax.axis_size("seq")
    if (row_count, seq_count) == (4, 8):
        first = jnp.concatenate([qkv_weight, out_weight], axis=1)[None]
        third = jnp.concatenate([proj_weight[256 * j : 256 * (j + 1)] for j in range(4)], axis=1)[
            None
        ]
        tables = (piece_table(True), piece_table(True), piece_table(False))
        return (
            gathered(first, (X, Y)),
            gathered(fc_weight[None], (X, Y)),
            gathered(third, (Y, X)),
        ), tables

    def full(shard):
        rows = lax.all_gather(shard, "row", axis=0, tiled=True)
        return lax.all_gather(rows, "seq", axis=1, tiled=True)

    def pieces(matrix):
        rows, cols = matrix.shape
        return (
            matrix.reshape(4, rows // 4, 8, cols // 8)
            .transpose(0, 2, 1, 3)
            .reshape(32, rows // 4, cols // 8)
        )

    proj = pieces(full(proj_weight)).reshape(32, 4, 256, 128)
    identity = jnp.arange(32, dtype=jnp.int32)
    return (
        jnp.concatenate([pieces(full(qkv_weight)), pieces(full(out_weight))], axis=2),
        pieces(full(fc_weight)),
        proj.transpose(0, 2, 1, 3).reshape(32, 256, 512),
    ), (identity,) * 3


def local(
    activations,
    cotangent,
    segment_ids,
    prefix_embed,
    adapt_in,
    adapt_in_bias,
    adapt_out,
    adapt_out_bias,
    ln1_gain,
    ln1_bias,
    qkv_weight,
    qkv_bias,
    out_weight,
    out_bias,
    ln2_gain,
    ln2_bias,
    fc_weight,
    fc_bias,
    proj_weight,
    proj_bias,
):
    batches, rows_dev, tok_dev, width = activations.shape
    tokens = batches * rows_dev * tok_dev
    assert tok_dev == 128 and rows_dev == 1 and lax.axis_size("seq") % 2 == 0
    x_side = lax.axis_index("seq") % 2

    x = activations.reshape(tokens, width)
    cot = cotangent.reshape(tokens, width)

    normal, _ = norm_parts(x.astype(F32))
    normed = (normal * ln1_gain.astype(F32) + ln1_bias.astype(F32)).astype(BF)
    ids = (segment_ids.reshape(1, tokens) + 1).astype(BF)
    sent = cat(normed, jnp.pad(ids, ((0, 7), (0, width - tokens))))
    h1 = moved(sent, "seq", 2)
    h2 = moved(h1, "seq", 2)
    o1 = swapped(h1, *X)
    r2 = swapped(jnp.where(x_side == 0, sent, h2), *X)
    seg = jnp.stack([part[tokens, :tokens] for part in (sent, o1, h1, r2, h2)])
    seg = seg.astype(F32).reshape(5, batches, tok_dev).transpose(1, 0, 2)

    (unit0, unit1, unit2), (tab0, tab1, tab2) = units_gathered(
        qkv_weight, out_weight, fc_weight, proj_weight
    )

    squashed = jnp.tanh(matmul_high(prefix_embed, adapt_in) + adapt_in_bias)
    prefix_kv = matmul_high(squashed, adapt_out) + adapt_out_bias
    count = prefix_kv.shape[0]
    prefix_low = jnp.pad(prefix_kv.astype(BF), ((0, 128 - count), (0, 0)))
    pk = prefix_low[:, :width].reshape(128, 8, 128).transpose(1, 0, 2)
    pv = prefix_low[:, width:].reshape(128, 8, 128).transpose(1, 0, 2)

    mixed, w_nat = qkv_call(
        tab0, (normed, o1, h1, r2, h2), unit0, qkv_bias.reshape(1, -1), tokens, width
    )
    att, probs = attend_call(seg, mixed, pk, pv, batches, tokens)
    middle, normed2, out_nat = middle_call(
        tab0,
        att,
        x,
        unit0,
        out_bias.reshape(1, -1),
        ln2_gain.reshape(1, -1),
        ln2_bias.reshape(1, -1),
        tokens,
    )
    hidden, slope = hidden_call(tab1, normed2, unit1, fc_bias.reshape(1, -1), tokens)
    grad_pre, proj_nat = grad_pre_call(tab2, cot, unit2, slope, tokens)
    grad_mid, grad_att = grad_middle_call(
        tab1, grad_pre, unit1, cot, middle, ln2_gain.reshape(1, -1), out_nat, tokens
    )

    owns, arrived, grad_pre_kv = [], [], 0.0
    for batch in range(batches):
        side, near, far, own, pre_kv = attend_back_call(
            batch, mixed, pk, pv, probs, grad_att, att, w_nat
        )
        grad_pre_kv = grad_pre_kv + pre_kv
        other = swapped(side, *X).astype(F32)
        to_far = far.astype(F32) + jnp.where(x_side == 1, other[1], 0.0)
        passing = moved(to_far.astype(BF), "seq", -2).astype(F32)
        to_near = near.astype(F32) + other[0] + passing
        landed = moved(to_near.astype(BF), "seq", -2).astype(F32)
        arrived.append(landed + jnp.where(x_side == 0, other[1], 0.0))
        owns.append(own)

    grad_normed = mm_nt(cat(*owns), w_nat) + cat(*arrived)
    in_grad = grad_mid + norm_back(x.astype(F32), grad_normed, ln1_gain.astype(F32))
    output = middle + mm(hidden, proj_nat) + proj_bias.astype(F32)

    total = summed_all(grad_pre_kv[:, :, :count])
    grad_kv = total.transpose(2, 0, 1, 3).reshape(count, 2 * width)
    adapt_out_grad = lax.dot_general(
        squashed,
        grad_kv,
        (((0,), (0,)), ((), ())),
        precision=lax.Precision.HIGHEST,
        preferred_element_type=F32,
    )
    grad_z = lax.dot_general(
        grad_kv,
        adapt_out,
        (((1,), (1,)), ((), ())),
        precision=lax.Precision.HIGHEST,
        preferred_element_type=F32,
    ) * (1.0 - squashed * squashed)
    adapt_in_grad = lax.dot_general(
        prefix_embed,
        grad_z,
        (((0,), (0,)), ((), ())),
        precision=lax.Precision.HIGHEST,
        preferred_element_type=F32,
    )
    prefix_grad = lax.dot_general(
        grad_z,
        adapt_in,
        (((1,), (1,)), ((), ())),
        precision=lax.Precision.HIGHEST,
        preferred_element_type=F32,
    )
    shape = activations.shape
    return (
        output.astype(BF).reshape(shape),
        in_grad.astype(BF).reshape(shape),
        prefix_grad,
        adapt_in_grad,
        jnp.sum(grad_z, axis=0),
        adapt_out_grad,
        jnp.sum(grad_kv, axis=0),
    )


def solution(mesh):
    rows = P(None, "row", "seq", None)
    split = P("row", "seq")
    placed = (
        rows,
        rows,
        P(None, "row", "seq"),
        P(),
        P(),
        P(),
        P(),
        P(),
        P(),
        P(),
        split,
        P(),
        split,
        P(),
        P(),
        P(),
        split,
        P(),
        split,
        P(),
    )
    return jax.shard_map(
        local,
        mesh=mesh,
        in_specs=placed,
        out_specs=(rows, rows, P(), P(), P(), P(), P()),
        check_vma=False,
    )
```

time: 1080 us -> 476 us (0.44)
  waiting for transfers between devices: 416 us -> 125 us
  starting transfers between devices: 275 us -> 65.5 us
  matrix products: 174 us -> 33.3 us
  Pallas kernels: 0 us -> 116 us
  blocking collectives: 87.4 us -> 0 us
  local copies, waits for them, and re-layouts: 52 us -> 89.7 us
  between operations: 26.1 us -> 2.05 us
    all_gather x6 -> x0, waiting for transfers between devices: 221 us -> none  [the longest x1 119 us: local(): lax.all_gather(lax.all_gather(proj_weight, 'row', axis=0, tiled=True), 's...]
    ppermute x66 -> x42, starting transfers between devices: 275 us -> 65.5 us  [the longest x34 46.9 us: swapped(): return lax.ppermute(value, axis, [(i, i ^ bit) for i in range(count)])]
    dot_general x57 -> x6, matrix products: 152 us -> 27 us  [the longest x1 9.13 us: mm(): return jnp.dot(left, right, preferred_element_type=F32)]
    pallas_call x0 -> x9, Pallas kernels: none -> 116 us  [the longest x3 47.7 us: attend_back_call(): pl.pallas_call(attend_back_kernel, grid=(1,), in_specs=[pl.BlockSpec((8,...]
    psum x1 -> x0, waiting for transfers between devices: 74.8 us -> none  [local(): lax.psum((local_grads[0], local_grads[1], local_grads[2], local_grads[3],...]
    psum x1 -> x0, blocking collectives: 67.4 us -> none  [local(): lax.psum((local_grads[0], local_grads[1], local_grads[2], local_grads[3],...]
    unnamed x491 -> x227, local copies, waits for them, and re-layouts: 28.7 us -> 67.5 us
    concatenate x0 -> x16, other arithmetic: none -> 20.1 us  [cat(): return jnp.concatenate(parts, axis=0)]
  transfers between devices with their start and end apart: 73 -> 42, of which waited for: 27 -> 18; matrix products, arithmetic and copies ran while one was open for 11% -> 23% of each run, Pallas kernels for 0% -> 12%
where the time goes in v1:
time: 476 us; the launch traced here: 469 us
  waiting for transfers between devices  125 us (26%)
  Pallas kernels  116 us (24%)
  local copies, waits for them, and re-layouts  89.7 us (19%)
  starting transfers between devices  65.5 us (14%)
  other arithmetic  37.7 us (8%)
  matrix products  33.3 us (7%)
    ppermute x34, waiting for transfers between devices, swapped(): return lax.ppermute(value, axis, [(i, i ^ bit) for i in range(count)])  101 us
    unnamed x227, local copies, waits for them, and re-layouts  67.5 us
    pallas_call x3, Pallas kernels, attend_back_call(): pl.pallas_call(attend_back_kernel, grid=(1,), in_specs=[pl.BlockSpec((8,...  47.7 us
    ppermute x34, starting transfers between devices, swapped(): return lax.ppermute(value, axis, [(i, i ^ bit) for i in range(count)])  46.9 us
    ppermute x8, waiting for transfers between devices, moved(): return lax.ppermute(value, axis, [(i, i + steps) for i in range(low, high)])  23.7 us
    pallas_call x1, Pallas kernels, attend_call(): pl.pallas_call(attend_kernel, grid=(batches,), in_specs=[pl.BlockSpec((1,...  20.9 us
    pallas_call x1, Pallas kernels, qkv_call(): pl.pallas_call(qkv_kernel, grid_spec=pltpu.PrefetchScalarGridSpec(num_sca...  20.2 us
    concatenate x16, other arithmetic, cat(): return jnp.concatenate(parts, axis=0)  20.1 us
  transfers between devices with their start and end apart: 42, of which 18 were waited for; matrix products, arithmetic and copies ran while one was open for 23% of the time, Pallas kernels for 12%

profile of v1, /device:TPU:0, one launch (start us, length us, event | category | flops | bytes accessed | tf_op | source)
XLA Modules:
  0.0 468.8 jit_solution(8003103610332026143)
XLA Ops:
  7.7 5.9 %collective-permute-start = (bf16[392,1024]{1,0:T(8,128)(2,1)}, bf16[392,1024]{1,0:T(8,128)(2,1)}, u32[]{:S(2)}, u32[]{:S(2)}) collective-permute-start(bf16[392,1024]{1,0:T(8,128)(2,1)} %fusion.14), channel_id=1, source_target_pairs={{0,2},{1,3},{2,4},{3,5},{4,6},{5,7},{8,10},{9,11},{10,12},{11,13},... | collective-permute-start | bytes 2408456 | tf_op jit(solution)/shard_map/ppermute | solution.py:48
  23.0 4.3 fusion.6
  30.5 9.0 %collective-permute-done.4 = bf16[1,256,512]{2,1,0:T(8,128)(2,1)S(1)} collective-permute-done((bf16[1,256,512]{2,1,0:T(8,128)(2,1)S(1)}, bf16[1,256,512]{2,1,0:T(8,128)(2,1)S(1)}, u32[]{:S(2)}, u32[]{:S(2)}) %collective-permute-start.4) | collective-permute-done | bytes 262176 | tf_op jit(solution)/shard_map/ppermute | solution.py:42
  54.5 15.8 %collective-permute-start.8 = (bf16[2,256,512]{2,1,0:T(8,128)(2,1)}, bf16[2,256,512]{2,1,0:T(8,128)(2,1)S(1)}, u32[]{:S(2)}, u32[]{:S(2)}) collective-permute-start(bf16[2,256,512]{2,1,0:T(8,128)(2,1)} %pad_maximum_fusion.12), channel_id=1, source_target_pairs={{0,2},{1,3},{2,0},{3,1},{4,6},{5,7},{6,4},{7,5},{8,10},{9,11},{10,... | collective-permute-start | bytes 1572872 | tf_op jit(solution)/shard_map/ppermute | solution.py:42
  79.8 3.5 collective-permute-done.8
  87.0 7.5 %collective-permute-done.16 = bf16[2,256,512]{2,1,0:T(8,128)(2,1)S(1)} collective-permute-done((bf16[2,256,512]{2,1,0:T(8,128)(2,1)S(1)}, bf16[2,256,512]{2,1,0:T(8,128)(2,1)S(1)}, u32[]{:S(2)}, u32[]{:S(2)}) %collective-permute-start.16) | collective-permute-done | bytes 524320 | tf_op jit(solution)/shard_map/ppermute | solution.py:42
  99.6 4.2 collective-permute-start.2
  110.0 21.9 %collective-permute-done.25 = bf16[2,256,512]{2,1,0:T(8,128)(2,1)S(1)} collective-permute-done((bf16[2,256,512]{2,1,0:T(8,128)(2,1)S(1)}, bf16[2,256,512]{2,1,0:T(8,128)(2,1)S(1)}, u32[]{:S(2)}, u32[]{:S(2)}) %collective-permute-start.25) | collective-permute-done | bytes 524320 | tf_op jit(solution)/shard_map/ppermute | solution.py:42
  134.9 2.6 pad_maximum_fusion
  137.5 16.8 %collective-permute-done.14 = bf16[4,256,512]{2,1,0:T(8,128)(2,1)S(1)} collective-permute-done((bf16[4,256,512]{2,1,0:T(8,128)(2,1)S(1)}, bf16[4,256,512]{2,1,0:T(8,128)(2,1)S(1)}, u32[]{:S(2)}, u32[]{:S(2)}) %collective-permute-start.14) | collective-permute-done | bytes 1048608 | tf_op jit(solution)/shard_map/ppermute | solution.py:42
  154.4 2.6 pad_maximum_fusion.2
  157.7 2.6 pad_maximum_fusion.4
  160.3 16.5 %collective-permute-done.10 = bf16[4,256,512]{2,1,0:T(8,128)(2,1)S(1)} collective-permute-done((bf16[4,256,512]{2,1,0:T(8,128)(2,1)S(1)}, bf16[4,256,512]{2,1,0:T(8,128)(2,1)S(1)}, u32[]{:S(2)}, u32[]{:S(2)}) %collective-permute-start.10) | collective-permute-done | bytes 1048608 | tf_op jit(solution)/shard_map/ppermute | solution.py:42
  177.4 14.6 %collective-permute-done.18 = bf16[4,256,512]{2,1,0:T(8,128)(2,1)S(1)} collective-permute-done((bf16[4,256,512]{2,1,0:T(8,128)(2,1)S(1)}, bf16[4,256,512]{2,1,0:T(8,128)(2,1)S(1)}, u32[]{:S(2)}, u32[]{:S(2)}) %collective-permute-start.18) | collective-permute-done | bytes 1048608 | tf_op jit(solution)/shard_map/ppermute | solution.py:42
  201.9 3.1 constant_dynamic-update-slice_fusion.4
  206.7 3.2 constant_dynamic-update-slice_fusion.13
  211.5 3.2 constant_dynamic-update-slice_fusion.22
  221.3 20.2 %qkv.1 = (bf16[24,5,384,128]{3,2,1,0:T(8,128)(2,1)}, bf16[1024,3072]{1,0:T(8,128)(2,1)S(1)}) custom-call(s32[32]{0:T(128)S(1)} %or.112.tab, bf16[384,1024]{1,0:T(8,128)(2,1)S(1)} %add_convert_fusion.2.own, bf16[392,1024]{1,0:T(8,128)(2,1)S(1)} %copy-done.23, bf16[392,1024]{1,0:T(8,128)(2,1)} %collective-permute-done.h1, bf16[392,1024]{1,0:T(8,128)(2,1)S(1)} %copy-done.25, ...), custom_call_target="tpu_custom_call" | custom-call | flops 8858370048 | bytes 20971520 | tf_op jit(solution)/shard_map/qkv/pallas_call | solution.py:139
  241.5 2.6 copy-done.6
  244.1 4.3 copy-done.1
  249.4 20.9 %attend.1 = (bf16[384,1024]{1,0:T(8,128)(2,1)S(1)}, bf16[3,8,768,256]{3,2,1,0:T(8,128)(2,1)S(1)}) custom-call(f32[3,5,128]{2,1,0:T(8,128)S(1)} %convert_bitcast_fusion.seg, bf16[24,5,384,128]{3,2,1,0:T(8,128)(2,1)S(1)} %copy-done.1, bf16[24,5,384,128]{3,2,1,0:T(8,128)(2,1)S(1)} %copy-done.1, bf16[24,5,384,128]{3,2,1,0:T(8,128)(2,1)S(1)} %copy-done.1, ...), custom_call_target="tpu_custom_call" | custom-call | flops 4831838208 | bytes 20971520 | tf_op jit(solution)/shard_map/attend/pallas_call | solution.py:215
  272.1 4.0 middle.1
  276.2 4.3 constant_dynamic-update-slice_fusion.9.w0.w1.w2.w3
  280.6 3.4 copy-done.3
  283.9 9.0 %hidden.1 = (bf16[384,4096]{1,0:T(8,128)(2,1)S(1)}, bf16[384,4096]{1,0:T(8,128)(2,1)S(1)}) custom-call(s32[32]{0:T(128)S(1)} %or.112.tab, bf16[384,1024]{1,0:T(8,128)(2,1)S(1)} %get-tuple-element.38.normed, bf16[32,256,512]{2,1,0:T(8,128)(2,1)S(1)} %copy-done.3, bf16[32,256,512]{2,1,0:T(8,128)(2,1)S(1)} %copy-done.3, bf16[32,256,512]{2,1,0:T(8,128)(2,1)S(1)} %copy-done.3, ...), custom_call_target="tpu_custom_call" | custom-call | flops 3221225472 | bytes 16777216 | tf_op jit(solution)/shard_map/hidden/pallas_call | solution.py:311
  293.0 4.2 constant_dynamic-update-slice_fusion.18.refs_0_.refs_1_.refs_2_.refs_3_.refs_4_.refs_5_.refs_6_.refs_7_
  297.2 3.5 copy-done.4
  300.7 5.2 %grad_pre.1 = (bf16[384,4096]{1,0:T(8,128)(2,1)S(1)}, bf16[4096,1024]{1,0:T(8,128)(2,1)S(1)}) custom-call(s32[32]{0:T(128)S(1)} %or.120.tab, bf16[384,1024]{1,0:T(8,128)(2,1)S(1)} %bitcast.127, bf16[32,256,512]{2,1,0:T(8,128)(2,1)S(1)} %copy-done.4, bf16[32,256,512]{2,1,0:T(8,128)(2,1)S(1)} %copy-done.4, bf16[32,256,512]{2,1,0:T(8,128)(2,1)S(1)} %copy-done.4, ...), custom_call_target="tpu_custom_call" | custom-call | flops 3221225472 | bytes 16777216 | tf_op jit(solution)/shard_map/grad_pre/pallas_call | solution.py:351
  307.5 3.3 copy-done.36
  314.5 8.6 %grad_middle.1 = (f32[384,1024]{1,0:T(8,128)S(1)}, bf16[384,1024]{1,0:T(8,128)(2,1)S(1)}) custom-call(s32[32]{0:T(128)S(1)} %or.112.tab, bf16[384,4096]{1,0:T(8,128)(2,1)S(1)} %copy-done.15, bf16[32,256,512]{2,1,0:T(8,128)(2,1)S(1)} %bitcast.113, bf16[32,256,512]{2,1,0:T(8,128)(2,1)S(1)} %bitcast.113, bf16[32,256,512]{2,1,0:T(8,128)(2,1)S(1)} %bitcast.113, ...), custom_call_target="tpu_custom_call" | custom-call | flops 4026531840 | bytes 16777216 | tf_op jit(solution)/shard_map/grad_middle/pallas_call | solution.py:403
  323.1 16.4 %attend_back.5 = (bf16[2,128,1024]{2,1,0:T(8,128)(2,1)S(1)}, bf16[128,1024]{1,0:T(8,128)(2,1)S(1)}, bf16[128,1024]{1,0:T(8,128)(2,1)S(1)}, bf16[128,3072]{1,0:T(8,128)(2,1)S(1)}, f32[2,8,16,128]{3,2,1,0:T(8,128)S(1)}) custom-call(bf16[24,5,384,128]{3,2,1,0:T(8,128)(2,1)} %get-tuple-element.35.q.k.v, bf16[24,5,384,128]{3,2,1,0:T(8,128)(2,1)} %get-tuple-element.35.q.k.v, ...), custom_call_target="tpu_custom_call" | custom-call | flops 5368709120 | bytes 16777216 | tf_op jit(solution)/shard_map/attend_back/pallas_call | solution.py:491
  342.6 15.4 %attend_back.4 = (bf16[2,128,1024]{2,1,0:T(8,128)(2,1)S(1)}, bf16[128,1024]{1,0:T(8,128)(2,1)S(1)}, bf16[128,1024]{1,0:T(8,128)(2,1)S(1)}, bf16[128,3072]{1,0:T(8,128)(2,1)S(1)}, f32[2,8,16,128]{3,2,1,0:T(8,128)S(1)}) custom-call(bf16[24,5,384,128]{3,2,1,0:T(8,128)(2,1)} %get-tuple-element.35.q.k.v, bf16[24,5,384,128]{3,2,1,0:T(8,128)(2,1)} %get-tuple-element.35.q.k.v, ...), custom_call_target="tpu_custom_call" | custom-call | flops 5368709120 | bytes 16777216 | tf_op jit(solution)/shard_map/attend_back/pallas_call | solution.py:491
  360.3 15.9 %attend_back.3 = (bf16[2,128,1024]{2,1,0:T(8,128)(2,1)S(1)}, bf16[128,1024]{1,0:T(8,128)(2,1)S(1)}, bf16[128,1024]{1,0:T(8,128)(2,1)S(1)}, bf16[128,3072]{1,0:T(8,128)(2,1)S(1)}, f32[2,8,16,128]{3,2,1,0:T(8,128)S(1)}) custom-call(bf16[24,5,384,128]{3,2,1,0:T(8,128)(2,1)} %get-tuple-element.35.q.k.v, bf16[24,5,384,128]{3,2,1,0:T(8,128)(2,1)} %get-tuple-element.35.q.k.v, ...), custom_call_target="tpu_custom_call" | custom-call | flops 5368709120 | bytes 16777216 | tf_op jit(solution)/shard_map/attend_back/pallas_call | solution.py:491
  381.6 4.1 collective-permute-done.38
  386.3 4.5 collective-permute-done.39
  395.8 3.8 collective-permute-start.41
  399.6 9.1 %add_convert_fusion.1 = bf16[384,1024]{1,0:T(8,128)(2,1)} fusion(f32[384,1024]{1,0:T(8,128)} %copy-done.18, bf16[384,4096]{1,0:T(8,128)(2,1)} %copy-done.37, bf16[4096,1024]{1,0:T(8,128)(2,1)} %copy-done.36, f32[1024]{0:T(1024)S(1)} %convert_element_type.130), kind=kOutput, calls=%fused_computation.25 | convolution fusion | flops 3222405120 | bytes 13897728 | tf_op jit(solution)/shard_map/dot_general | solution.py:23
  409.5 4.2 fusion.34
  413.7 5.2 %fusion.36 = f32[512,2048]{1,0:T(8,128)} fusion(f32[10,512]{1,0:T(8,128)S(1)} %copy-done.75, f32[10,2048]{1,0:T(8,128)S(1)} %bitcast.130), kind=kOutput, calls=%fused_computation.129 | convolution fusion | flops 125829120 | bytes 4296704 | tf_op jit(solution)/shard_map/dot_general | solution.py:657
  421.3 3.1 convolution_bitcast_fusion
  424.5 2.9 copy.47
  435.5 4.6 collective-permute-done.35
  441.6 4.1 collective-permute-done.32
  447.1 4.2 collective-permute-done.29
  453.1 3.9 collective-permute-done.36
  457.0 4.2 collective-permute-done.33
  461.3 2.7 collective-permute-done.30
  464.2 3.0 fusion.31
  (362 shorter events, 124.5 us)
Async XLA Ops:
  7.7 91.9 %collective-permute-start = (bf16[392,1024]{1,0:T(8,128)(2,1)}, bf16[392,1024]{1,0:T(8,128)(2,1)}, u32[]{:S(2)}, u32[]{:S(2)}) collective-permute-start(bf16[392,1024]{1,0:T(8,128)(2,1)} %fusion.14), channel_id=1, source_target_pairs={{0,2},{1,3},{2,4},{3,5},{4,6},{5,7},{8,10},{9,11},{10,12},{11,13},... | collective-permute-start | bytes 2408456 | tf_op jit(solution)/shard_map/ppermute | solution.py:48
  13.7 25.8 %collective-permute-start.4 = (bf16[1,256,512]{2,1,0:T(8,128)(2,1)S(1)}, bf16[1,256,512]{2,1,0:T(8,128)(2,1)S(1)}, u32[]{:S(2)}, u32[]{:S(2)}) collective-permute-start(bf16[1,256,512]{2,1,0:T(8,128)(2,1)S(1)} %maximum_bitcast_fusion), channel_id=1, source_target_pairs={{0,4},{1,5},{2,6},{3,7},{4,0},{5,1},{6,2},{7,3},{8,12},{9,13},{10,... | collective-permute-start | bytes 786440 | tf_op jit(solution)/shard_map/ppermute | solution.py:42
  15.5 54.8 %collective-permute-start.12 = (bf16[1,256,512]{2,1,0:T(8,128)(2,1)}, bf16[1,256,512]{2,1,0:T(8,128)(2,1)}, u32[]{:S(2)}, u32[]{:S(2)}) collective-permute-start(bf16[1,256,512]{2,1,0:T(8,128)(2,1)} %bitcast.15), channel_id=1, source_target_pairs={{0,4},{1,5},{2,6},{3,7},{4,0},{5,1},{6,2},{7,3},{8,12},{9,13},{10,... | collective-permute-start | bytes 786440 | tf_op jit(solution)/shard_map/ppermute | solution.py:42
  18.1 53.8 %collective-permute-start.20 = (bf16[1,256,512]{2,1,0:T(8,128)(2,1)}, bf16[1,256,512]{2,1,0:T(8,128)(2,1)}, u32[]{:S(2)}, u32[]{:S(2)}) collective-permute-start(bf16[1,256,512]{2,1,0:T(8,128)(2,1)} %maximum_bitcast_fusion.1), channel_id=1, source_target_pairs={{0,4},{1,5},{2,6},{3,7},{4,0},{5,1},{6,2},{7,3},{8,12},{9,13},{10,... | collective-permute-start | bytes 786440 | tf_op jit(solution)/shard_map/ppermute | solution.py:42
  40.4 33.3 %collective-permute-start.5 = (bf16[2,256,512]{2,1,0:T(8,128)(2,1)}, bf16[2,256,512]{2,1,0:T(8,128)(2,1)}, u32[]{:S(2)}, u32[]{:S(2)}) collective-permute-start(bf16[2,256,512]{2,1,0:T(8,128)(2,1)} %pad_maximum_fusion.12), channel_id=1, source_target_pairs={{0,1},{1,0},{2,3},{3,2},{4,5},{5,4},{6,7},{7,6},{8,9},{9,8},{10,11... | collective-permute-start | bytes 1572872 | tf_op jit(solution)/shard_map/ppermute | solution.py:42
  54.5 28.8 %collective-permute-start.8 = (bf16[2,256,512]{2,1,0:T(8,128)(2,1)}, bf16[2,256,512]{2,1,0:T(8,128)(2,1)S(1)}, u32[]{:S(2)}, u32[]{:S(2)}) collective-permute-start(bf16[2,256,512]{2,1,0:T(8,128)(2,1)} %pad_maximum_fusion.12), channel_id=1, source_target_pairs={{0,2},{1,3},{2,0},{3,1},{4,6},{5,7},{6,4},{7,5},{8,10},{9,11},{10,... | collective-permute-start | bytes 1572872 | tf_op jit(solution)/shard_map/ppermute | solution.py:42
  71.3 14.0 %collective-permute-start.13 = (bf16[2,256,512]{2,1,0:T(8,128)(2,1)S(1)}, bf16[2,256,512]{2,1,0:T(8,128)(2,1)S(1)}, u32[]{:S(2)}, u32[]{:S(2)}) collective-permute-start(bf16[2,256,512]{2,1,0:T(8,128)(2,1)S(1)} %pad_maximum_fusion.13), channel_id=1, source_target_pairs={{0,1},{1,0},{2,3},{3,2},{4,5},{5,4},{6,7},{7,6},{8,9},{9,8},{10,11... | collective-permute-start | bytes 1572872 | tf_op jit(solution)/shard_map/ppermute | solution.py:42
  71.9 22.6 %collective-permute-start.16 = (bf16[2,256,512]{2,1,0:T(8,128)(2,1)S(1)}, bf16[2,256,512]{2,1,0:T(8,128)(2,1)S(1)}, u32[]{:S(2)}, u32[]{:S(2)}) collective-permute-start(bf16[2,256,512]{2,1,0:T(8,128)(2,1)S(1)} %pad_maximum_fusion.13), channel_id=1, source_target_pairs={{0,2},{1,3},{2,0},{3,1},{4,6},{5,7},{6,4},{7,5},{8,10},{9,11},{10,... | collective-permute-start | bytes 1572872 | tf_op jit(solution)/shard_map/ppermute | solution.py:42
  73.8 24.2 %collective-permute-start.21 = (bf16[2,256,512]{2,1,0:T(8,128)(2,1)S(1)}, bf16[2,256,512]{2,1,0:T(8,128)(2,1)S(1)}, u32[]{:S(2)}, u32[]{:S(2)}) collective-permute-start(bf16[2,256,512]{2,1,0:T(8,128)(2,1)S(1)} %pad_maximum_fusion.14), channel_id=1, source_target_pairs={{0,16},{8,24},{16,0},{24,8},{1,17},{9,25},{17,1},{25,9},{2,18},{10... | collective-permute-start | bytes 1572872 | tf_op jit(solution)/shard_map/ppermute | solution.py:42
  83.3 112.0 %copy-start.48 = (bf16[2,256,512]{2,1,0:T(8,128)(2,1)}, bf16[2,256,512]{2,1,0:T(8,128)(2,1)S(1)}, u32[]{:S(2)}) copy-start(bf16[2,256,512]{2,1,0:T(8,128)(2,1)S(1)} %collective-permute-done.8) | copy-start | bytes 1572868
  83.3 22.0 %collective-permute-start.24 = (bf16[2,256,512]{2,1,0:T(8,128)(2,1)S(1)}, bf16[2,256,512]{2,1,0:T(8,128)(2,1)S(1)}, u32[]{:S(2)}, u32[]{:S(2)}) collective-permute-start(bf16[2,256,512]{2,1,0:T(8,128)(2,1)S(1)} %pad_maximum_fusion.14), channel_id=1, source_target_pairs={{0,2},{1,3},{2,0},{3,1},{4,6},{5,7},{6,4},{7,5},{8,10},{9,11},{10,... | collective-permute-start | bytes 1572872 | tf_op jit(solution)/shard_map/ppermute | solution.py:42
  85.3 22.3 %collective-permute-start.9 = (bf16[2,256,512]{2,1,0:T(8,128)(2,1)S(1)}, bf16[2,256,512]{2,1,0:T(8,128)(2,1)S(1)}, u32[]{:S(2)}, u32[]{:S(2)}) collective-permute-start(bf16[2,256,512]{2,1,0:T(8,128)(2,1)S(1)} %collective-permute-done.8), channel_id=1, source_target_pairs={{0,1},{1,0},{2,3},{3,2},{4,5},{5,4},{6,7},{7,6},{8,9},{9,8},{10,11... | collective-permute-start | bytes 1572872 | tf_op jit(solution)/shard_map/ppermute | solution.py:42
  94.5 102.3 %copy-start.50 = (bf16[2,256,512]{2,1,0:T(8,128)(2,1)}, bf16[2,256,512]{2,1,0:T(8,128)(2,1)S(1)}, u32[]{:S(2)}) copy-start(bf16[2,256,512]{2,1,0:T(8,128)(2,1)S(1)} %collective-permute-done.16) | copy-start | bytes 1572868
  94.5 39.6 %collective-permute-start.6 = (bf16[4,256,512]{2,1,0:T(8,128)(2,1)S(1)}, bf16[4,256,512]{2,1,0:T(8,128)(2,1)S(1)}, u32[]{:S(2)}, u32[]{:S(2)}) collective-permute-start(bf16[4,256,512]{2,1,0:T(8,128)(2,1)S(1)} %pad_maximum_fusion.6), channel_id=1, source_target_pairs={{0,16},{8,24},{16,0},{24,8},{1,17},{9,25},{17,1},{25,9},{2,18},{10... | collective-permute-start | bytes 3145736 | tf_op jit(solution)/shard_map/ppermute | solution.py:42
  97.9 11.0 %collective-permute-start.17 = (bf16[2,256,512]{2,1,0:T(8,128)(2,1)S(1)}, bf16[2,256,512]{2,1,0:T(8,128)(2,1)S(1)}, u32[]{:S(2)}, u32[]{:S(2)}) collective-permute-start(bf16[2,256,512]{2,1,0:T(8,128)(2,1)S(1)} %collective-permute-done.16), channel_id=1, source_target_pairs={{0,1},{1,0},{2,3},{3,2},{4,5},{5,4},{6,7},{7,6},{8,9},{9,8},{10,11... | collective-permute-start | bytes 1572872 | tf_op jit(solution)/shard_map/ppermute | solution.py:42
  99.6 32.9 %collective-permute-start.2 = (bf16[392,1024]{1,0:T(8,128)(2,1)}, bf16[392,1024]{1,0:T(8,128)(2,1)S(1)}, u32[]{:S(2)}, u32[]{:S(2)}) collective-permute-start(bf16[392,1024]{1,0:T(8,128)(2,1)} %collective-permute-done.h1), channel_id=1, source_target_pairs={{0,2},{1,3},{2,4},{3,5},{4,6},{5,7},{8,10},{9,11},{10,12},{11,13},... | collective-permute-start | bytes 2408456 | tf_op jit(solution)/shard_map/ppermute | solution.py:48
  105.3 93.5 %copy-start.52 = (bf16[2,256,512]{2,1,0:T(8,128)(2,1)}, bf16[2,256,512]{2,1,0:T(8,128)(2,1)S(1)}, u32[]{:S(2)}) copy-start(bf16[2,256,512]{2,1,0:T(8,128)(2,1)S(1)} %collective-permute-done.24) | copy-start | bytes 1572868
  105.3 26.6 %collective-permute-start.25 = (bf16[2,256,512]{2,1,0:T(8,128)(2,1)S(1)}, bf16[2,256,512]{2,1,0:T(8,128)(2,1)S(1)}, u32[]{:S(2)}, u32[]{:S(2)}) collective-permute-start(bf16[2,256,512]{2,1,0:T(8,128)(2,1)S(1)} %collective-permute-done.24), channel_id=1, source_target_pairs={{0,16},{8,24},{16,0},{24,8},{1,17},{9,25},{17,1},{25,9},{2,18},{10... | collective-permute-start | bytes 1572872 | tf_op jit(solution)/shard_map/ppermute | solution.py:42
  107.7 87.6 %copy-start.54 = (bf16[2,256,512]{2,1,0:T(8,128)(2,1)}, bf16[2,256,512]{2,1,0:T(8,128)(2,1)S(1)}, u32[]{:S(2)}) copy-start(bf16[2,256,512]{2,1,0:T(8,128)(2,1)S(1)} %collective-permute-done.9) | copy-start | bytes 1572868
  107.7 46.7 %collective-permute-start.14 = (bf16[4,256,512]{2,1,0:T(8,128)(2,1)S(1)}, bf16[4,256,512]{2,1,0:T(8,128)(2,1)S(1)}, u32[]{:S(2)}, u32[]{:S(2)}) collective-permute-start(bf16[4,256,512]{2,1,0:T(8,128)(2,1)S(1)} %pad_maximum_fusion.8), channel_id=1, source_target_pairs={{0,16},{8,24},{16,0},{24,8},{1,17},{9,25},{17,1},{25,9},{2,18},{10... | collective-permute-start | bytes 3145736 | tf_op jit(solution)/shard_map/ppermute | solution.py:42
  109.0 87.9 %copy-start.56 = (bf16[2,256,512]{2,1,0:T(8,128)(2,1)}, bf16[2,256,512]{2,1,0:T(8,128)(2,1)S(1)}, u32[]{:S(2)}) copy-start(bf16[2,256,512]{2,1,0:T(8,128)(2,1)S(1)} %collective-permute-done.17) | copy-start | bytes 1572868
  109.0 48.5 %collective-permute-start.22 = (bf16[4,256,512]{2,1,0:T(8,128)(2,1)S(1)}, bf16[4,256,512]{2,1,0:T(8,128)(2,1)S(1)}, u32[]{:S(2)}, u32[]{:S(2)}) collective-permute-start(bf16[4,256,512]{2,1,0:T(8,128)(2,1)S(1)} %pad_maximum_fusion.10), channel_id=1, source_target_pairs={{0,1},{1,0},{2,3},{3,2},{4,5},{5,4},{6,7},{7,6},{8,9},{9,8},{10,11... | collective-permute-start | bytes 3145736 | tf_op jit(solution)/shard_map/ppermute | solution.py:42
  131.9 66.9 %copy-start.58 = (bf16[2,256,512]{2,1,0:T(8,128)(2,1)}, bf16[2,256,512]{2,1,0:T(8,128)(2,1)S(1)}, u32[]{:S(2)}) copy-start(bf16[2,256,512]{2,1,0:T(8,128)(2,1)S(1)} %collective-permute-done.25) | copy-start | bytes 1572868
  131.9 25.1 %collective-permute-start.1 = (bf16[392,1024]{1,0:T(8,128)(2,1)}, bf16[392,1024]{1,0:T(8,128)(2,1)S(1)}, u32[]{:S(2)}, u32[]{:S(2)}) collective-permute-start(bf16[392,1024]{1,0:T(8,128)(2,1)} %collective-permute-done.h1), channel_id=1, source_target_pairs={{0,1},{1,0},{2,3},{3,2},{4,5},{5,4},{6,7},{7,6},{8,9},{9,8},{10,11... | collective-permute-start | bytes 2408456 | tf_op jit(solution)/shard_map/ppermute | solution.py:42
  132.5 44.3 %collective-permute-start.10 = (bf16[4,256,512]{2,1,0:T(8,128)(2,1)S(1)}, bf16[4,256,512]{2,1,0:T(8,128)(2,1)S(1)}, u32[]{:S(2)}, u32[]{:S(2)}) collective-permute-start(bf16[4,256,512]{2,1,0:T(8,128)(2,1)S(1)} %pad_maximum_fusion.7), channel_id=1, source_target_pairs={{0,16},{8,24},{16,0},{24,8},{1,17},{9,25},{17,1},{25,9},{2,18},{10... | collective-permute-start | bytes 3145736 | tf_op jit(solution)/shard_map/ppermute | solution.py:42
  134.1 57.8 %collective-permute-start.18 = (bf16[4,256,512]{2,1,0:T(8,128)(2,1)S(1)}, bf16[4,256,512]{2,1,0:T(8,128)(2,1)S(1)}, u32[]{:S(2)}, u32[]{:S(2)}) collective-permute-start(bf16[4,256,512]{2,1,0:T(8,128)(2,1)S(1)} %pad_maximum_fusion.9), channel_id=1, source_target_pairs={{0,16},{8,24},{16,0},{24,8},{1,17},{9,25},{17,1},{25,9},{2,18},{10... | collective-permute-start | bytes 3145736 | tf_op jit(solution)/shard_map/ppermute | solution.py:42
  154.3 47.1 %collective-permute-start.7 = (bf16[8,256,512]{2,1,0:T(8,128)(2,1)}, bf16[8,256,512]{2,1,0:T(8,128)(2,1)}, u32[]{:S(2)}, u32[]{:S(2)}) collective-permute-start(bf16[8,256,512]{2,1,0:T(8,128)(2,1)} %pad_maximum_fusion), channel_id=1, source_target_pairs={{0,8},{8,0},{16,24},{24,16},{1,9},{9,1},{17,25},{25,17},{2,10},{10... | collective-permute-start | bytes 6291464 | tf_op jit(solution)/shard_map/ppermute | solution.py:42
  156.9 41.4 %collective-permute-start.26 = (bf16[4,256,512]{2,1,0:T(8,128)(2,1)S(1)}, bf16[4,256,512]{2,1,0:T(8,128)(2,1)S(1)}, u32[]{:S(2)}, u32[]{:S(2)}) collective-permute-start(bf16[4,256,512]{2,1,0:T(8,128)(2,1)S(1)} %pad_maximum_fusion.11), channel_id=1, source_target_pairs={{0,1},{1,0},{2,3},{3,2},{4,5},{5,4},{6,7},{7,6},{8,9},{9,8},{10,11... | collective-permute-start | bytes 3145736 | tf_op jit(solution)/shard_map/ppermute | solution.py:42
  157.5 49.2 %collective-permute-start.15 = (bf16[8,256,512]{2,1,0:T(8,128)(2,1)}, bf16[8,256,512]{2,1,0:T(8,128)(2,1)}, u32[]{:S(2)}, u32[]{:S(2)}) collective-permute-start(bf16[8,256,512]{2,1,0:T(8,128)(2,1)} %pad_maximum_fusion.2), channel_id=1, source_target_pairs={{0,8},{8,0},{16,24},{24,16},{1,9},{9,1},{17,25},{25,17},{2,10},{10... | collective-permute-start | bytes 6291464 | tf_op jit(solution)/shard_map/ppermute | solution.py:42
  176.8 23.6 %collective-permute-start.3 = (bf16[392,1024]{1,0:T(8,128)(2,1)S(1)}, bf16[392,1024]{1,0:T(8,128)(2,1)S(1)}, u32[]{:S(2)}, u32[]{:S(2)}) collective-permute-start(bf16[392,1024]{1,0:T(8,128)(2,1)S(1)} %broadcast_select_fusion), channel_id=1, source_target_pairs={{0,1},{1,0},{2,3},{3,2},{4,5},{5,4},{6,7},{7,6},{8,9},{9,8},{10,11... | collective-permute-start | bytes 2408456 | tf_op jit(solution)/shard_map/ppermute | solution.py:42
  191.9 19.6 %collective-permute-start.23 = (bf16[8,256,512]{2,1,0:T(8,128)(2,1)}, bf16[8,256,512]{2,1,0:T(8,128)(2,1)}, u32[]{:S(2)}, u32[]{:S(2)}) collective-permute-start(bf16[8,256,512]{2,1,0:T(8,128)(2,1)} %pad_maximum_fusion.4), channel_id=1, source_target_pairs={{0,8},{8,0},{16,24},{24,16},{1,9},{9,1},{17,25},{25,17},{2,10},{10... | collective-permute-start | bytes 6291464 | tf_op jit(solution)/shard_map/ppermute | solution.py:42
  198.4 20.7 %collective-permute-start.11 = (bf16[8,256,512]{2,1,0:T(8,128)(2,1)}, bf16[8,256,512]{2,1,0:T(8,128)(2,1)}, u32[]{:S(2)}, u32[]{:S(2)}) collective-permute-start(bf16[8,256,512]{2,1,0:T(8,128)(2,1)} %pad_maximum_fusion.1), channel_id=1, source_target_pairs={{0,8},{8,0},{16,24},{24,16},{1,9},{9,1},{17,25},{25,17},{2,10},{10... | collective-permute-start | bytes 6291464 | tf_op jit(solution)/shard_map/ppermute | solution.py:42
  200.4 75.8 %collective-permute-start.19 = (bf16[8,256,512]{2,1,0:T(8,128)(2,1)}, bf16[8,256,512]{2,1,0:T(8,128)(2,1)}, u32[]{:S(2)}, u32[]{:S(2)}) collective-permute-start(bf16[8,256,512]{2,1,0:T(8,128)(2,1)} %pad_maximum_fusion.3), channel_id=1, source_target_pairs={{0,8},{8,0},{16,24},{24,16},{1,9},{9,1},{17,25},{25,17},{2,10},{10... | collective-permute-start | bytes 6291464 | tf_op jit(solution)/shard_map/ppermute | solution.py:42
  201.5 91.5 %collective-permute-start.27 = (bf16[8,256,512]{2,1,0:T(8,128)(2,1)}, bf16[8,256,512]{2,1,0:T(8,128)(2,1)}, u32[]{:S(2)}, u32[]{:S(2)}) collective-permute-start(bf16[8,256,512]{2,1,0:T(8,128)(2,1)} %pad_maximum_fusion.5), channel_id=1, source_target_pairs={{0,8},{8,0},{16,24},{24,16},{1,9},{9,1},{17,25},{25,17},{2,10},{10... | collective-permute-start | bytes 6291464 | tf_op jit(solution)/shard_map/ppermute | solution.py:42
  378.6 1.3 collective-permute-start.37
  379.9 5.8 %collective-permute-start.38 = (f32[2,8,10,128]{3,2,1,0:T(8,128)S(1)}, f32[2,8,10,128]{3,2,1,0:T(8,128)S(1)}, u32[]{:S(2)}, u32[]{:S(2)}) collective-permute-start(f32[2,8,10,128]{3,2,1,0:T(8,128)S(1)} %add.166), channel_id=1, source_target_pairs={{0,16},{8,24},{16,0},{24,8},{1,17},{9,25},{17,1},{25,9},{2,18},{10... | collective-permute-start | bytes 245768 | tf_op jit(solution)/shard_map/ppermute | solution.py:42
  385.7 5.0 %collective-permute-start.39 = (f32[2,8,10,128]{3,2,1,0:T(8,128)S(1)}, f32[2,8,10,128]{3,2,1,0:T(8,128)S(1)}, u32[]{:S(2)}, u32[]{:S(2)}) collective-permute-start(f32[2,8,10,128]{3,2,1,0:T(8,128)S(1)} %add.167), channel_id=1, source_target_pairs={{0,1},{1,0},{2,3},{3,2},{4,5},{5,4},{6,7},{7,6},{8,9},{9,8},{10,11... | collective-permute-start | bytes 245768 | tf_op jit(solution)/shard_map/ppermute | solution.py:42
  390.8 5.0 %collective-permute-start.40 = (f32[2,8,10,128]{3,2,1,0:T(8,128)S(1)}, f32[2,8,10,128]{3,2,1,0:T(8,128)S(1)}, u32[]{:S(2)}, u32[]{:S(2)}) collective-permute-start(f32[2,8,10,128]{3,2,1,0:T(8,128)S(1)} %add.168), channel_id=1, source_target_pairs={{0,2},{1,3},{2,0},{3,1},{4,6},{5,7},{6,4},{7,5},{8,10},{9,11},{10,... | collective-permute-start | bytes 245768 | tf_op jit(solution)/shard_map/ppermute | solution.py:42
  392.3 35.1 %collective-permute-start.34 = (bf16[2,128,1024]{2,1,0:T(8,128)(2,1)}, bf16[2,128,1024]{2,1,0:T(8,128)(2,1)}, u32[]{:S(2)}, u32[]{:S(2)}) collective-permute-start(bf16[2,128,1024]{2,1,0:T(8,128)(2,1)} %copy-done.46), channel_id=1, source_target_pairs={{0,1},{1,0},{2,3},{3,2},{4,5},{5,4},{6,7},{7,6},{8,9},{9,8},{10,11... | collective-permute-start | bytes 1572872 | tf_op jit(solution)/shard_map/ppermute | solution.py:42
  392.8 37.4 %collective-permute-start.31 = (bf16[2,128,1024]{2,1,0:T(8,128)(2,1)}, bf16[2,128,1024]{2,1,0:T(8,128)(2,1)}, u32[]{:S(2)}, u32[]{:S(2)}) collective-permute-start(bf16[2,128,1024]{2,1,0:T(8,128)(2,1)} %copy-done.45), channel_id=1, source_target_pairs={{0,1},{1,0},{2,3},{3,2},{4,5},{5,4},{6,7},{7,6},{8,9},{9,8},{10,11... | collective-permute-start | bytes 1572872 | tf_op jit(solution)/shard_map/ppermute | solution.py:42
  394.3 38.6 %collective-permute-start.28 = (bf16[2,128,1024]{2,1,0:T(8,128)(2,1)}, bf16[2,128,1024]{2,1,0:T(8,128)(2,1)}, u32[]{:S(2)}, u32[]{:S(2)}) collective-permute-start(bf16[2,128,1024]{2,1,0:T(8,128)(2,1)} %copy-done.44), channel_id=1, source_target_pairs={{0,1},{1,0},{2,3},{3,2},{4,5},{5,4},{6,7},{7,6},{8,9},{9,8},{10,11... | collective-permute-start | bytes 1572872 | tf_op jit(solution)/shard_map/ppermute | solution.py:42
  395.8 12.9 %collective-permute-start.41 = (f32[2,8,10,128]{3,2,1,0:T(8,128)S(1)}, f32[2,8,10,128]{3,2,1,0:T(8,128)S(1)}, u32[]{:S(2)}, u32[]{:S(2)}) collective-permute-start(f32[2,8,10,128]{3,2,1,0:T(8,128)S(1)} %add.169), channel_id=1, source_target_pairs={{0,4},{1,5},{2,6},{3,7},{4,0},{5,1},{6,2},{7,3},{8,12},{9,13},{10,... | collective-permute-start | bytes 245768 | tf_op jit(solution)/shard_map/ppermute | solution.py:42
  428.8 11.2 %collective-permute-start.35 = (bf16[128,1024]{1,0:T(8,128)(2,1)S(1)}, bf16[128,1024]{1,0:T(8,128)(2,1)S(1)}, u32[]{:S(2)}, u32[]{:S(2)}) collective-permute-start(bf16[128,1024]{1,0:T(8,128)(2,1)S(1)} %fusion.24), channel_id=1, source_target_pairs={{2,0},{3,1},{4,2},{5,3},{6,4},{7,5},{10,8},{11,9},{12,10},{13,11},... | collective-permute-start | bytes 786440 | tf_op jit(solution)/shard_map/ppermute | solution.py:48
  431.5 14.2 %collective-permute-start.32 = (bf16[128,1024]{1,0:T(8,128)(2,1)S(1)}, bf16[128,1024]{1,0:T(8,128)(2,1)S(1)}, u32[]{:S(2)}, u32[]{:S(2)}) collective-permute-start(bf16[128,1024]{1,0:T(8,128)(2,1)S(1)} %fusion.25), channel_id=1, source_target_pairs={{2,0},{3,1},{4,2},{5,3},{6,4},{7,5},{10,8},{11,9},{12,10},{13,11},... | collective-permute-start | bytes 786440 | tf_op jit(solution)/shard_map/ppermute | solution.py:48
  434.2 17.1 %collective-permute-start.29 = (bf16[128,1024]{1,0:T(8,128)(2,1)S(1)}, bf16[128,1024]{1,0:T(8,128)(2,1)S(1)}, u32[]{:S(2)}, u32[]{:S(2)}) collective-permute-start(bf16[128,1024]{1,0:T(8,128)(2,1)S(1)} %fusion.26), channel_id=1, source_target_pairs={{2,0},{3,1},{4,2},{5,3},{6,4},{7,5},{10,8},{11,9},{12,10},{13,11},... | collective-permute-start | bytes 786440 | tf_op jit(solution)/shard_map/ppermute | solution.py:48
  440.2 16.7 %collective-permute-start.36 = (bf16[128,1024]{1,0:T(8,128)(2,1)S(1)}, bf16[128,1024]{1,0:T(8,128)(2,1)S(1)}, u32[]{:S(2)}, u32[]{:S(2)}) collective-permute-start(bf16[128,1024]{1,0:T(8,128)(2,1)S(1)} %fusion.17), channel_id=1, source_target_pairs={{2,0},{3,1},{4,2},{5,3},{6,4},{7,5},{10,8},{11,9},{12,10},{13,11},... | collective-permute-start | bytes 786440 | tf_op jit(solution)/shard_map/ppermute | solution.py:48
  445.8 15.4 %collective-permute-start.33 = (bf16[128,1024]{1,0:T(8,128)(2,1)S(1)}, bf16[128,1024]{1,0:T(8,128)(2,1)S(1)}, u32[]{:S(2)}, u32[]{:S(2)}) collective-permute-start(bf16[128,1024]{1,0:T(8,128)(2,1)S(1)} %fusion.20), channel_id=1, source_target_pairs={{2,0},{3,1},{4,2},{5,3},{6,4},{7,5},{10,8},{11,9},{12,10},{13,11},... | collective-permute-start | bytes 786440 | tf_op jit(solution)/shard_map/ppermute | solution.py:48
  451.5 12.5 %collective-permute-start.30 = (bf16[128,1024]{1,0:T(8,128)(2,1)S(1)}, bf16[128,1024]{1,0:T(8,128)(2,1)S(1)}, u32[]{:S(2)}, u32[]{:S(2)}) collective-permute-start(bf16[128,1024]{1,0:T(8,128)(2,1)S(1)} %fusion.23), channel_id=1, source_target_pairs={{2,0},{3,1},{4,2},{5,3},{6,4},{7,5},{10,8},{11,9},{12,10},{13,11},... | collective-permute-start | bytes 786440 | tf_op jit(solution)/shard_map/ppermute | solution.py:48
  (95 other events, 748.1 us)
